TPU v7x, 256 devices: a whole 4x4x8 slice. The times are simulated.
256 devices in a mesh: section: 8 (over z), tp: 8 (over y, core), dp: 4 (over x).
Axes of the slice: x: 4, y: 4, z: 8, core: 2. Of those that a mesh axis runs over, the one named last changes fastest.
Arguments:
- images: bfloat16 [32, 1024, 3200], P(('section', 'dp')), may hold values from -6 to 6
- counts: int32 [32], P(('section', 'dp')), may hold values from 256 to 1024, as said below
- norm_gain: float32 [3200], replicated, may hold values from 0.25 to 1.75
- w_qkv: bfloat16 [3, 3200, 3072], P(None, ('section', 'dp'), 'tp'), may hold values from -1 to 1
- w_out: bfloat16 [3072, 3200], P('tp', ('section', 'dp')), may hold values from -1 to 1
- layer_scale: float32 [3200], P('tp'), may hold values from 0.5 to 1.5
- order: int32 [4, 8], replicated, may hold values from 0 to 7, each once within a row
Outputs:
- vision_tokens: bfloat16 [4, 8, 1024, 3200], P('dp', None, 'section', 'tp')
Inputs may be any that keep to these rules, and one draw needn't show every extreme that they name: `counts`: some block in every draw is full. `order`: each row is a permutation.
All inputs are finite; a program needn't handle non-finite values.
Results may differ from a plain program's by a relative error of at most 0.02.
Values may be sent and summed in bfloat16 or wider, within the bound.
No kernel may reach another device: no remote copies, remote signals or barrier semaphores. Data moves between devices by JAX's collectives and lax.ppermute only.
A program may use at most 128 MiB of HBM per device.

v0:
```python
import functools
import math

import jax
import jax.numpy as jnp
from jax import lax
from jax.experimental import pallas as pl
from jax.experimental.pallas import tpu as pltpu
from jax.sharding import PartitionSpec as P

HD = 128
BF = jnp.bfloat16
F32 = jnp.float32
ORDER = (4, 3, 5, 2, 6, 1, 7, 0)
GROUPS = ((0, 4), (4, 8))


def norm_body(x_ref, gain_ref, plain, by_dp):
    x = x_ref[...].astype(F32)
    scale = lax.rsqrt(jnp.mean(x * x, axis=-1, keepdims=True) + 1e-06)
    y = (x * scale * gain_ref[...]).astype(BF)
    plain[...] = y
    for s in range(8):
        for d in range(4):
            by_dp[d, :, s * 100 : s * 100 + 100] = y[:, (s * 4 + d) * 100 : (s * 4 + d) * 100 + 100]


def normalise(x, gain):
    rows, wide = x.shape
    tile = 128
    return pl.pallas_call(
        norm_body,
        grid=(rows // tile,),
        in_specs=[
            pl.BlockSpec((tile, wide), lambda r: (r, 0)),
            pl.BlockSpec((1, wide), lambda r: (0, 0)),
        ],
        out_specs=[
            pl.BlockSpec((tile, wide), lambda r: (r, 0)),
            pl.BlockSpec((4, tile, 800), lambda r: (0, r, 0)),
        ],
        out_shape=[
            jax.ShapeDtypeStruct((rows, wide), BF),
            jax.ShapeDtypeStruct((4, rows, 800), BF),
        ],
        compiler_params=pltpu.CompilerParams(vmem_limit_bytes=16 * 2**20),
        cost_estimate=pl.CostEstimate(flops=30_000_000, bytes_accessed=20_000_000, transcendentals=1024),
    )(x, gain[None])


def early_body(at_ref, x_ref, own_top, own_low, back_top, back_low, ahead_top, ahead_low, out_ref):
    total = jnp.zeros(out_ref.shape, F32)
    for k, (top, low) in enumerate(((own_top, own_low), (back_top, back_low), (ahead_top, ahead_low))):
        total += jnp.dot(x_ref[at_ref[k], :, :400], top[...], preferred_element_type=F32)
        total += jnp.dot(x_ref[at_ref[k], :, 400:], low[...], preferred_element_type=F32)
    out_ref[...] = total


def early(at, by_dp, *halves):
    rows, deep = by_dp.shape[1:]
    wide = halves[0].shape[1]
    tile = 256
    half = pl.BlockSpec((deep // 2, wide), lambda r, a: (0, 0))
    return pl.pallas_call(
        early_body,
        grid_spec=pltpu.PrefetchScalarGridSpec(
            num_scalar_prefetch=1,
            grid=(rows // tile,),
            in_specs=[
                pl.BlockSpec((4, tile, deep), lambda r, a: (0, r, 0)),
            ]
            + [half] * 6,
            out_specs=pl.BlockSpec((tile, wide), lambda r, a: (r, 0)),
        ),
        out_shape=jax.ShapeDtypeStruct((rows, wide), F32),
        compiler_params=pltpu.CompilerParams(vmem_limit_bytes=58 * 2**20),
        cost_estimate=pl.CostEstimate(
            flops=6 * rows * deep * wide, bytes_accessed=15_000_000, transcendentals=0
        ),
    )(at, by_dp, *halves)


def attend_tile(live_keys, query, key, vt, out_ref):
    keys = key.shape[0]
    rows = query.shape[0]
    live = lax.broadcasted_iota(jnp.int32, (keys, rows), 0) < live_keys
    factor = math.log2(math.e) / math.sqrt(HD)
    for h in range(out_ref.shape[0] // HD):
        at = slice(h * HD, h * HD + HD)
        scores = lax.dot_general(
            key[:, at], query[:, at], (((1,), (1,)), ((), ())), preferred_element_type=F32
        )
        scores = jnp.where(live, scores, -jnp.inf)
        top = jnp.max(scores, axis=0, keepdims=True)
        expo = jnp.exp2((scores - top) * factor)
        total = jnp.sum(expo, axis=0, keepdims=True)
        context = jnp.dot(vt[at, :], expo.astype(BF), preferred_element_type=F32)
        out_ref[at, :] = (context / total).astype(BF)


def late_body(at_ref, sums, x_ref, top, low, normed, w_ref, qk_ref, vt_ref, ctx_ref, qk, vt):
    step = pl.program_id(0)
    tile, wide = sums.shape
    narrow = wide // 2

    @pl.when(step < 4)
    def _():
        total = sums[...] + jnp.dot(x_ref[0, :, :400], top[...], preferred_element_type=F32)
        total += jnp.dot(x_ref[0, :, 400:], low[...], preferred_element_type=F32)
        qk_ref[...] = total.astype(BF)
        value = jnp.dot(normed[...], w_ref[...], preferred_element_type=F32)
        vt_ref[...] = value.T.astype(BF)

    for r in range(4):

        @pl.when(step == r)
        def _():
            qk[r * tile : r * tile + tile] = qk_ref[...]
            vt[:, r * tile : r * tile + tile] = vt_ref[...]

    @pl.when(step >= 4)
    def _():
        rows = [
            pl.ds(pl.multiple_of(at_ref[5 + 2 * (step - 4) + i] * 128, 128), 128) for i in range(2)
        ]
        query = jnp.concatenate([qk[rows[0], :narrow], qk[rows[1], :narrow]], axis=0)
        attend_tile(at_ref[4], query, qk[:, narrow:], vt, ctx_ref)


def late(at, sums, by_dp, top, low, normed, w_v):
    rows, wide = sums.shape
    deep, tall = by_dp.shape[2], normed.shape[1]
    narrow = w_v.shape[1]
    tile = rows // 4
    half = pl.BlockSpec((deep // 2, wide), lambda r, a: (0, 0))

    def upto(r):
        return jnp.minimum(r, 3)

    return pl.pallas_call(
        late_body,
        grid_spec=pltpu.PrefetchScalarGridSpec(
            num_scalar_prefetch=1,
            grid=(6,),
            in_specs=[
                pl.BlockSpec((tile, wide), lambda r, a: (upto(r), 0)),
                pl.BlockSpec((1, tile, deep), lambda r, a: (a[3], upto(r), 0)),
                half,
                half,
                pl.BlockSpec((tile, tall), lambda r, a: (upto(r), 0)),
                pl.BlockSpec((tall, narrow), lambda r, a: (0, 0)),
            ],
            out_specs=[
                pl.BlockSpec((tile, wide), lambda r, a: (upto(r), 0)),
                pl.BlockSpec((narrow, tile), lambda r, a: (0, upto(r))),
                pl.BlockSpec((narrow, 256), lambda r, a: (0, jnp.maximum(r - 4, 0))),
            ],
            scratch_shapes=[pltpu.VMEM((rows, wide), BF), pltpu.VMEM((narrow, rows), BF)],
        ),
        out_shape=[
            jax.ShapeDtypeStruct((rows, wide), BF),
            jax.ShapeDtypeStruct((narrow, rows), BF),
            jax.ShapeDtypeStruct((narrow, 512), BF),
        ],
        compiler_params=pltpu.CompilerParams(vmem_limit_bytes=58 * 2**20),
        cost_estimate=pl.CostEstimate(
            flops=2 * rows * (deep * wide + tall * narrow) + 2 * rows * rows * narrow,
            bytes_accessed=18_000_000,
            transcendentals=rows * rows * 3 // 2,
        ),
    )(at, sums, by_dp, top, low, normed, w_v)


def attend_body(info_ref, q0_ref, q1_ref, k_ref, vt_ref, out_ref):
    query = jnp.concatenate([q0_ref[...], q1_ref[...]], axis=0)
    attend_tile(info_ref[0], query, k_ref[...], vt_ref, out_ref)


def attend(info, rows, qk, vt):
    wide, keys = vt.shape
    return pl.pallas_call(
        attend_body,
        grid_spec=pltpu.PrefetchScalarGridSpec(
            num_scalar_prefetch=1,
            grid=(rows // 256,),
            in_specs=[
                pl.BlockSpec((128, wide), lambda r, i: (i[1 + 2 * r], 0)),
                pl.BlockSpec((128, wide), lambda r, i: (i[2 + 2 * r], 0)),
                pl.BlockSpec((keys, wide), lambda r, i: (0, 1)),
                pl.BlockSpec((wide, keys), lambda r, i: (0, 0)),
            ],
            out_specs=pl.BlockSpec((wide, 256), lambda r, i: (0, r)),
        ),
        out_shape=jax.ShapeDtypeStruct((wide, rows), BF),
        compiler_params=pltpu.CompilerParams(vmem_limit_bytes=16 * 2**20),
        cost_estimate=pl.CostEstimate(
            flops=4 * rows * keys * wide, bytes_accessed=4_000_000, transcendentals=rows * keys * 3
        ),
    )(info, qk, qk, qk, vt)


def project_body(first, info_ref, own_ctx, back, ahead, far, sibling, w_hbm, own_ref, scale_ref, out_ref, w, sems):
    copies = [
        pltpu.make_async_copy(w_hbm.at[info_ref[j]], w.at[j], sems.at[j]) for j in range(8)
    ]
    for copy in copies:
        copy.start()
    near = (own_ctx, back, ahead, far)
    total = None
    for j in range(8):
        copies[j].wait()
        ctx = near[j][...] if j < 4 else sibling[j - 4]
        term = jnp.dot(w[j], ctx, preferred_element_type=F32)
        total = term if total is None else total + term
    total = scale_ref[...] * total
    for c in range(out_ref.shape[0]):
        row = lax.broadcasted_iota(jnp.int32, (1, 128), 1) + info_ref[9 + c]
        value = own_ref[first + c].astype(F32) + total[:, c * 128 : c * 128 + 128]
        out_ref[c] = jnp.where(row < info_ref[8], value, 0.0).astype(BF)


def project(first, info, near, sibling, w8, own, scale):
    chunks, tall = 4, own.shape[1]
    whole = pl.BlockSpec(memory_space=pltpu.VMEM)
    return pl.pallas_call(
        functools.partial(project_body, first),
        in_specs=[pl.BlockSpec(memory_space=pltpu.SMEM)]
        + [whole] * 5
        + [pl.BlockSpec(memory_space=pl.ANY)]
        + [whole] * 2,
        out_specs=whole,
        out_shape=jax.ShapeDtypeStruct((chunks, tall, 128), BF),
        scratch_shapes=[pltpu.VMEM(w8.shape, BF), pltpu.SemaphoreType.DMA((8,))],
        compiler_params=pltpu.CompilerParams(vmem_limit_bytes=16 * 2**20),
        cost_estimate=pl.CostEstimate(
            flops=2 * chunks * tall * 384 * 8 * 128, bytes_accessed=6_000_000, transcendentals=0
        ),
    )(info, *near, sibling, w8, own, scale)


def deliver_body(info_ref, order_ref, *refs):
    out_ref = refs[8]
    for k in range(8):
        source = (info_ref[0] - k + 8) % 8
        slot = 0
        for j in range(8):
            slot = jnp.where(order_ref[info_ref[1], j] == source, j, slot)
        out_ref[slot] = refs[k][...]


def deliver(info, order, pieces):
    whole = pl.BlockSpec(memory_space=pltpu.VMEM)
    scalars = pl.BlockSpec(memory_space=pltpu.SMEM)
    return pl.pallas_call(
        deliver_body,
        in_specs=[scalars, scalars] + [whole] * 8,
        out_specs=whole,
        out_shape=jax.ShapeDtypeStruct((8,) + pieces[0].shape, BF),
        compiler_params=pltpu.CompilerParams(vmem_limit_bytes=16 * 2**20),
    )(info, order, *pieces)


def around(x, axis, step, size):
    return lax.ppermute(x, axis, [(i, (i + step) % size) for i in range(size)])


def place(parts, places, count):
    out = jnp.zeros((count,) + parts[0].shape, parts[0].dtype)
    for part, at in zip(parts, places):
        out = lax.dynamic_update_slice(out, part[None], (at, 0, 0))
    return out.reshape(count * parts[0].shape[0], parts[0].shape[1])


def shards(images, counts, norm_gain, w_qkv, w_out, layer_scale, order):
    sec, tp, dp = (lax.axis_index(a) for a in ("section", "tp", "dp"))
    y, core = tp // 2, tp % 2
    whole = images[0]
    count = counts[0]
    share = layer_scale.shape[0]

    w_b = jnp.concatenate([w_qkv[0], w_qkv[1]], axis=1)
    block_b = lax.all_gather(w_b, "section", axis=0, tiled=False)
    own_top, own_low = block_b[:4].reshape(400, 768), block_b[4:].reshape(400, 768)

    w_o = lax.ppermute(
        w_out.T, ("section", "tp"), [(s * 8 + t, t * 8 + s) for s in range(8) for t in range(8)]
    )
    w_a = jnp.concatenate([w_qkv[2], w_o], axis=1)
    parts = (w_a, around(w_a, "dp", 1, 4), around(w_a, "dp", -1, 4), around(w_a, "dp", 2, 4))
    block_a = place(parts, (dp, (dp + 3) % 4, (dp + 1) % 4, (dp + 2) % 4), 4)
    w_v = lax.all_gather(block_a[:, :384], "section", axis=0, tiled=True)
    rel = (sec + jnp.array(ORDER, jnp.int32)) % 8
    own = lax.dynamic_slice_in_dim(whole, tp * share, share, 1)
    own = jnp.take(own.reshape(8, 128, share).transpose(0, 2, 1), rel, axis=0, mode="clip")
    normed, by_dp = normalise(whole, norm_gain)
    own_top, own_low, block_o, normed, by_dp, own = lax.optimization_barrier(
        (own_top, own_low, block_a[:, 384:], normed, by_dp, own)
    )
    w8 = lax.all_gather(block_o, "section", axis=0, tiled=False)

    back_top = around(own_top, "dp", 1, 4)
    ahead_low = around(own_low, "dp", -1, 4)
    back_low = around(own_low, "dp", 1, 4)
    ahead_top = around(own_top, "dp", -1, 4)
    far_top = around(back_top, "dp", 1, 4)
    far_low = around(ahead_low, "dp", -1, 4)

    at = jnp.stack([dp, (dp + 3) % 4, (dp + 1) % 4, (dp + 2) % 4]).astype(jnp.int32)
    at = jnp.concatenate([at, counts, rel[:4]])
    sums = early(at, by_dp, own_top, own_low, back_top, back_low, ahead_top, ahead_low)
    qk, value_t, ctx0 = late(at, sums, by_dp, far_top, far_low, normed, w_v)

    near_groups = [2 * ((y + off) % 4) + core for off in (0, 3, 1, 2)]
    far_groups = [2 * ((y + off) % 4) + 1 - core for off in (0, 3, 1, 2)]
    scale = layer_scale[:, None]

    received = {}
    info = jnp.stack(near_groups + far_groups + [count]).astype(jnp.int32)
    infos = [jnp.concatenate([info, rel[first:last] * 128]) for first, last in GROUPS]
    ask = jnp.concatenate([counts, rel[4:]])

    def both_ways(up, down):
        return around(up, "tp", 2, 8), around(down, "tp", -2, 8)

    def shared(near):
        return lax.ppermute(jnp.stack(near), "tp", [(i, i ^ 1) for i in range(8)])

    def sent(encoded, first, last):
        for j in range(first, last):
            k = ORDER[j]
            piece = encoded[j - first]
            received[k] = around(piece, "section", k, 8) if k else piece

    back0, ahead0 = both_ways(ctx0, ctx0)
    ctx1 = attend(ask, 512, qk, value_t)
    up, down = both_ways(
        jnp.concatenate([ctx1, back0[:192]], axis=0), jnp.concatenate([ctx1, ahead0[192:]], axis=0)
    )
    near0 = (ctx0, back0, ahead0, jnp.concatenate([up[384:], down[384:]], axis=0))
    back1, ahead1 = up[:384], down[:384]
    top, low = both_ways(back1[:192], ahead1[192:])
    near1 = (ctx1, back1, ahead1, jnp.concatenate([top, low], axis=0))
    sibling0 = shared(near0)
    encoded0 = project(0, infos[0], near0, sibling0, w8, own, scale)
    sent(encoded0, 0, 4)
    sibling1 = shared(near1)
    encoded1 = project(4, infos[1], near1, sibling1, w8, own, scale)
    sent(encoded1, 4, 8)
    arranged = deliver(jnp.stack([sec, dp]).astype(jnp.int32), order, [received[k] for k in range(8)])
    return arranged.transpose(0, 2, 1)[None]


def solution(mesh):
    in_specs = (
        P(("section", "dp"), None, None),
        P(("section", "dp")),
        P(),
        P(None, ("section", "dp"), "tp"),
        P("tp", ("section", "dp")),
        P("tp"),
        P(),
    )
    out_specs = P("dp", None, "section", "tp")
    return jax.shard_map(shards, mesh=mesh, in_specs=in_specs, out_specs=out_specs, check_vma=False)
```

profile of v0, /device:TPU:1, one launch (start us, length us, event | category | flops | bytes accessed | tf_op | source)
XLA Modules:
  0.0 196.5 jit_solution(15613692065808373795)
XLA Ops:
  6.5 1.0 slice_bitcast_fusion.8
  7.5 0.7 maximum_bitcast_fusion
  8.3 4.9 %collective-permute-start = (bf16[100,384]{1,0:T(8,128)(2,1)}, bf16[100,384]{1,0:T(8,128)(2,1)S(1)}, u32[]{:S(2)}, u32[]{:S(2)}) collective-permute-start(bf16[100,384]{1,0:T(8,128)(2,1)} %bitcast.76), channel_id=1, source_target_pairs={{0,0},{4,32},{8,64},{12,96},{16,128},{20,160},{24,192},{28,224},{3... | collective-permute-start | bytes 230408 | tf_op jit(solution)/shard_map/ppermute | solution.py:285
  13.2 2.3 %collective-permute-done = bf16[100,384]{1,0:T(8,128)(2,1)S(1)} collective-permute-done((bf16[100,384]{1,0:T(8,128)(2,1)}, bf16[100,384]{1,0:T(8,128)(2,1)S(1)}, u32[]{:S(2)}, u32[]{:S(2)}) %collective-permute-start) | collective-permute-done | bytes 76832 | tf_op jit(solution)/shard_map/ppermute | solution.py:285
  15.5 1.6 collective-permute-start.1
  17.1 1.4 collective-permute-start.2
  18.5 1.6 collective-permute-start.3
  20.2 1.4 collective-permute-done.1
  21.7 2.3 %collective-permute-done.2 = bf16[100,768]{1,0:T(8,128)(2,1)S(1)} collective-permute-done((bf16[100,768]{1,0:T(8,128)(2,1)S(1)}, bf16[100,768]{1,0:T(8,128)(2,1)S(1)}, u32[]{:S(2)}, u32[]{:S(2)}) %collective-permute-start.2) | collective-permute-done | bytes 153632 | tf_op jit(solution)/shard_map/ppermute | solution.py:264
  24.0 1.7 collective-permute-done.3
  25.8 0.9 fusion.3
  26.8 1.8 constant_dynamic-slice_fusion
  28.6 0.6 copy.16
  29.3 0.7 gather_fusion
  30.0 2.9 %copy-done.4 = bf16[1,1024,3200]{2,1,0:T(8,128)(2,1)S(1)} copy-done((bf16[1,1024,3200]{2,1,0:T(8,128)(2,1)S(1)}, bf16[1,1024,3200]{2,1,0:T(8,128)(2,1)}, u32[]{:S(2)}) %copy-start.4) | copy-done | bytes 6553624
  32.9 7.2 %shard_map.82 = (bf16[1024,3200]{1,0:T(8,128)(2,1)S(1)}, bf16[4,1024,800]{2,1,0:T(8,128)(2,1)S(1)}) custom-call(bf16[1024,3200]{1,0:T(8,128)(2,1)S(1)} %bitcast.67, f32[1,3200]{1,0:T(1,128)S(1)} %broadcast_in_dim.33.gain_ref), custom_call_target="tpu_custom_call" | custom-call | flops 30000000 | bytes 20000000 | tf_op jit(solution)/shard_map/pallas_call | solution.py:31
  40.1 3.0 %copy-done = bf16[4,1024,800]{2,1,0:T(8,128)(2,1)} copy-done((bf16[4,1024,800]{2,1,0:T(8,128)(2,1)}, bf16[4,1024,800]{2,1,0:T(8,128)(2,1)S(1)}, u32[]{:S(2)}) %copy-start) | copy-done | bytes 6553624
  43.1 2.7 %copy-done.5 = bf16[1024,3200]{1,0:T(8,128)(2,1)} copy-done((bf16[1024,3200]{1,0:T(8,128)(2,1)}, bf16[1024,3200]{1,0:T(8,128)(2,1)S(1)}, u32[]{:S(2)}) %copy-start.5) | copy-done | bytes 6553624
  45.8 2.5 %all-gather.11.cloned.1.call-done = bf16[8,100,768]{2,1,0:T(8,128)(2,1)} async-done(((bf16[1,100,768]{2,1,0:T(8,128)(2,1)}), bf16[8,100,768]{2,1,0:T(8,128)(2,1)}) %all-gather.11.cloned.1.call-update) | async-done | bytes 1228816 | tf_op jit(solution)/shard_map/all_gather | solution.py:282
  48.3 1.4 fusion.2
  49.9 1.4 collective-permute-start.4
  51.2 1.4 collective-permute-start.7
  52.7 2.6 %collective-permute-start.6 = (bf16[400,768]{1,0:T(8,128)(2,1)S(1)}, bf16[400,768]{1,0:T(8,128)(2,1)}, u32[]{:S(2)}, u32[]{:S(2)}) collective-permute-start(bf16[400,768]{1,0:T(8,128)(2,1)S(1)} %reshape.35.own_top), channel_id=1, source_target_pairs={{0,3},{1,0},{2,1},{3,2},{4,7},{5,4},{6,5},{7,6},{8,11},{9,8},{10,9... | collective-permute-start | bytes 1843208 | tf_op jit(solution)/shard_map/ppermute | solution.py:264
  55.3 6.6 %collective-permute-done.4.back_top = bf16[400,768]{1,0:T(8,128)(2,1)S(1)} collective-permute-done((bf16[400,768]{1,0:T(8,128)(2,1)S(1)}, bf16[400,768]{1,0:T(8,128)(2,1)S(1)}, u32[]{:S(2)}, u32[]{:S(2)}) %collective-permute-start.4) | collective-permute-done | bytes 614432 | tf_op jit(solution)/shard_map/ppermute | solution.py:264
  61.9 0.2 collective-permute-start.8
  62.1 2.5 %collective-permute-start.9 = (bf16[400,768]{1,0:T(8,128)(2,1)S(1)}, bf16[400,768]{1,0:T(8,128)(2,1)}, u32[]{:S(2)}, u32[]{:S(2)}) collective-permute-start(bf16[400,768]{1,0:T(8,128)(2,1)S(1)} %collective-permute-done.7.ahead_low), channel_id=1, source_target_pairs={{0,3},{1,0},{2,1},{3,2},{4,7},{5,4},{6,5},{7,6},{8,11},{9,8},{10,9... | collective-permute-start | bytes 1843208 | tf_op jit(solution)/shard_map/ppermute | solution.py:264
  65.3 0.6 concatenate.34.at_ref
  65.9 9.2 %collective-permute-done.5.back_low = bf16[400,768]{1,0:T(8,128)(2,1)} collective-permute-done((bf16[400,768]{1,0:T(8,128)(2,1)S(1)}, bf16[400,768]{1,0:T(8,128)(2,1)}, u32[]{:S(2)}, u32[]{:S(2)}) %collective-permute-start.5) | collective-permute-done | bytes 614432 | tf_op jit(solution)/shard_map/ppermute | solution.py:264
  75.2 10.3 %shard_map.83.sums = f32[1024,768]{1,0:T(8,128)} custom-call(s32[9]{0:T(128)} %concatenate.34.at_ref, bf16[4,1024,800]{2,1,0:T(8,128)(2,1)} %copy-done, bf16[400,768]{1,0:T(8,128)(2,1)} %copy-done.11, bf16[400,768]{1,0:T(8,128)(2,1)} %copy-done.12, bf16[400,768]{1,0:T(8,128)(2,1)} %copy-done.13, bf16[400,768]{1,0:T(8,128)(2,1)} %collective-permute-done.5.back_low, ...), custom_call_target="tpu_custom_call" | custom-call | flops 3774873600 | bytes 15000000 | tf_op jit(solution)/shard_map/pallas_call | solution.py:64
  85.5 2.8 %collective-permute-done.8.top = bf16[400,768]{1,0:T(8,128)(2,1)} collective-permute-done((bf16[400,768]{1,0:T(8,128)(2,1)S(1)}, bf16[400,768]{1,0:T(8,128)(2,1)}, u32[]{:S(2)}, u32[]{:S(2)}) %collective-permute-start.8) | collective-permute-done | bytes 614432 | tf_op jit(solution)/shard_map/ppermute | solution.py:264
  88.3 3.2 %all-gather.7.cloned.1.call-done.w_ref = bf16[3200,384]{1,0:T(8,128)(2,1)} async-done(((bf16[400,384]{1,0:T(8,128)(2,1)}), bf16[3200,384]{1,0:T(8,128)(2,1)}) %all-gather.7.cloned.1.call-update) | async-done | bytes 2457616 | tf_op jit(solution)/shard_map/all_gather | solution.py:291
  91.5 16.1 %shard_map.84 = (bf16[1024,768]{1,0:T(8,128)(2,1)}, bf16[384,1024]{1,0:T(8,128)(2,1)}, bf16[384,512]{1,0:T(8,128)(2,1)}) custom-call(s32[9]{0:T(128)} %concatenate.34.at_ref, f32[1024,768]{1,0:T(8,128)} %shard_map.83.sums, bf16[4,1024,800]{2,1,0:T(8,128)(2,1)} %copy-done, bf16[400,768]{1,0:T(8,128)(2,1)} %collective-permute-done.8.top, ...), custom_call_target="tpu_custom_call" | custom-call | flops 4580179968 | bytes 18000000 | tf_op jit(solution)/shard_map/pallas_call | solution.py:140
  107.6 1.1 collective-permute-start.10
  108.7 9.2 %collective-permute-start.12 = (bf16[384,512]{1,0:T(8,128)(2,1)}, bf16[384,512]{1,0:T(8,128)(2,1)S(1)}, u32[]{:S(2)}, u32[]{:S(2)}) collective-permute-start(bf16[384,512]{1,0:T(8,128)(2,1)} %get-tuple-element.24.own_ctx), channel_id=1, source_target_pairs={{0,24},{4,28},{8,0},{12,4},{16,8},{20,12},{24,16},{28,20},{1,25},{... | collective-permute-start | bytes 1179656 | tf_op jit(solution)/shard_map/ppermute | solution.py:264
  118.0 1.4 copy-done.1
  119.4 1.1 copy-done.9
  120.5 5.1 %shard_map.85.own_ctx = bf16[384,512]{1,0:T(8,128)(2,1)S(1)} custom-call(s32[5]{0:T(128)S(1)} %pad_add_fusion.1.info_ref, bf16[1024,768]{1,0:T(8,128)(2,1)S(1)} %copy-done.1, bf16[1024,768]{1,0:T(8,128)(2,1)S(1)} %copy-done.1, bf16[1024,768]{1,0:T(8,128)(2,1)S(1)} %copy-done.1, bf16[384,1024]{1,0:T(8,128)(2,1)S(1)} %copy-done.9), custom_call_target="tpu_custom_call" | custom-call | flops 805306368 | bytes 4000000 | tf_op jit(solution)/shard_map/pallas_call | solution.py:181
  126.0 0.7 collective-permute-start.11
  126.7 2.1 %collective-permute-start.13 = (bf16[576,512]{1,0:T(8,128)(2,1)S(1)}, bf16[576,512]{1,0:T(8,128)(2,1)S(1)}, u32[]{:S(2)}, u32[]{:S(2)}) collective-permute-start(bf16[576,512]{1,0:T(8,128)(2,1)S(1)} %get-tuple-element.49), channel_id=1, source_target_pairs={{0,24},{4,28},{8,0},{12,4},{16,8},{20,12},{24,16},{28,20},{1,25},{... | collective-permute-start | bytes 1769480 | tf_op jit(solution)/shard_map/ppermute | solution.py:264
  128.8 11.1 %collective-permute-done.11 = bf16[576,512]{1,0:T(8,128)(2,1)S(1)} collective-permute-done((bf16[576,512]{1,0:T(8,128)(2,1)S(1)}, bf16[576,512]{1,0:T(8,128)(2,1)S(1)}, u32[]{:S(2)}, u32[]{:S(2)}) %collective-permute-start.11) | collective-permute-done | bytes 589856 | tf_op jit(solution)/shard_map/ppermute | solution.py:264
  140.0 0.8 fusion.1
  140.8 1.4 pad_maximum_fusion.1
  142.1 3.2 %collective-permute-start.18 = (bf16[4,384,512]{2,1,0:T(8,128)(2,1)}, bf16[4,384,512]{2,1,0:T(8,128)(2,1)}, u32[]{:S(2)}, u32[]{:S(2)}) collective-permute-start(bf16[4,384,512]{2,1,0:T(8,128)(2,1)} %pad_maximum_fusion.1), channel_id=1, source_target_pairs={{0,4},{4,0},{8,12},{12,8},{16,20},{20,16},{24,28},{28,24},{1,5},{5... | collective-permute-start | bytes 4718600 | tf_op jit(solution)/shard_map/ppermute | solution.py:326
  145.3 0.5 collective-permute-start.14
  145.8 2.2 %collective-permute-start.15 = (bf16[192,512]{1,0:T(8,128)(2,1)S(1)}, bf16[192,512]{1,0:T(8,128)(2,1)S(1)}, u32[]{:S(2)}, u32[]{:S(2)}) collective-permute-start(bf16[192,512]{1,0:T(8,128)(2,1)S(1)} %get-tuple-element.34), channel_id=1, source_target_pairs={{0,24},{4,28},{8,0},{12,4},{16,8},{20,12},{24,16},{28,20},{1,25},{... | collective-permute-start | bytes 589832 | tf_op jit(solution)/shard_map/ppermute | solution.py:264
  148.0 0.8 slice_bitcast_fusion.11
  148.8 4.2 %collective-permute-done.14 = bf16[192,512]{1,0:T(8,128)(2,1)S(1)} collective-permute-done((bf16[192,512]{1,0:T(8,128)(2,1)S(1)}, bf16[192,512]{1,0:T(8,128)(2,1)S(1)}, u32[]{:S(2)}, u32[]{:S(2)}) %collective-permute-start.14) | collective-permute-done | bytes 196640 | tf_op jit(solution)/shard_map/ppermute | solution.py:264
  153.1 1.4 pad_maximum_fusion
  154.5 0.8 collective-permute-start.16
  155.6 1.7 copy-done.2
  157.3 1.0 copy-done.8
  158.3 4.5 %shard_map.87 = bf16[4,400,128]{2,1,0:T(8,128)(2,1)S(1)} custom-call(s32[13]{0:T(128)S(1)} %concatenate.40.info_ref, bf16[384,512]{1,0:T(8,128)(2,1)S(1)} %copy-done.6, bf16[384,512]{1,0:T(8,128)(2,1)S(1)} %collective-permute-done.10.back, bf16[384,512]{1,0:T(8,128)(2,1)S(1)} %collective-permute-done.12.ahead, bf16[384,512]{1,0:T(8,128)(2,1)S(1)} %copy-done.8, ...), custom_call_target="tpu_custom_call" | custom-call | flops 1258291200 | bytes 6000000 | tf_op jit(solution)/shard_map/pallas_call | solution.py:225
  162.9 4.1 %collective-permute-start.20 = (bf16[400,128]{1,0:T(8,128)(2,1)S(1)}, bf16[400,128]{1,0:T(8,128)(2,1)S(1)}, u32[]{:S(2)}, u32[]{:S(2)}) collective-permute-start(bf16[400,128]{1,0:T(8,128)(2,1)S(1)} %get-tuple-element.45), channel_id=1, source_target_pairs={{0,96},{32,128},{64,160},{96,192},{128,224},{160,0},{192,32},{224,... | collective-permute-start | bytes 307208 | tf_op jit(solution)/shard_map/ppermute | solution.py:264
  167.0 2.6 %collective-permute-start.21 = (bf16[400,128]{1,0:T(8,128)(2,1)S(1)}, bf16[400,128]{1,0:T(8,128)(2,1)S(1)}, u32[]{:S(2)}, u32[]{:S(2)}) collective-permute-start(bf16[400,128]{1,0:T(8,128)(2,1)S(1)} %get-tuple-element.44), channel_id=1, source_target_pairs={{0,128},{32,160},{64,192},{96,224},{128,0},{160,32},{192,64},{224,... | collective-permute-start | bytes 307208 | tf_op jit(solution)/shard_map/ppermute | solution.py:264
  169.6 0.7 collective-permute-start.22
  170.3 4.3 %shard_map.86 = bf16[4,400,128]{2,1,0:T(8,128)(2,1)S(1)} custom-call(s32[13]{0:T(128)S(1)} %concatenate.32.info_ref, bf16[384,512]{1,0:T(8,128)(2,1)S(1)} %shard_map.85.own_ctx, bf16[384,512]{1,0:T(8,128)(2,1)S(1)} %get-tuple-element.36.back, bf16[384,512]{1,0:T(8,128)(2,1)S(1)} %copy-done.7, bf16[384,512]{1,0:T(8,128)(2,1)S(1)} %constant_dynamic-update-slice_fusion.far, ...), custom_call_target="tpu_custom_call" | custom-call | flops 1258291200 | bytes 6000000 | tf_op jit(solution)/shard_map/pallas_call | solution.py:225
  174.7 1.3 collective-permute-start.17
  176.0 2.3 %collective-permute-start.23 = (bf16[400,128]{1,0:T(8,128)(2,1)S(1)}, bf16[400,128]{1,0:T(8,128)(2,1)S(1)}, u32[]{:S(2)}, u32[]{:S(2)}) collective-permute-start(bf16[400,128]{1,0:T(8,128)(2,1)S(1)} %get-tuple-element.40), channel_id=1, source_target_pairs={{0,192},{32,224},{64,0},{96,32},{128,64},{160,96},{192,128},{224,1... | collective-permute-start | bytes 307208 | tf_op jit(solution)/shard_map/ppermute | solution.py:264
  178.4 1.8 collective-permute-done.20.refs_3_
  180.2 1.8 collective-permute-done.22.refs_5_
  182.1 3.3 %collective-permute-done.17.refs_1_ = bf16[400,128]{1,0:T(8,128)(2,1)S(1)} collective-permute-done((bf16[400,128]{1,0:T(8,128)(2,1)S(1)}, bf16[400,128]{1,0:T(8,128)(2,1)S(1)}, u32[]{:S(2)}, u32[]{:S(2)}) %collective-permute-start.17) | collective-permute-done | bytes 102432 | tf_op jit(solution)/shard_map/ppermute | solution.py:264
  185.3 2.3 %collective-permute-done.23.refs_6_ = bf16[400,128]{1,0:T(8,128)(2,1)S(1)} collective-permute-done((bf16[400,128]{1,0:T(8,128)(2,1)S(1)}, bf16[400,128]{1,0:T(8,128)(2,1)S(1)}, u32[]{:S(2)}, u32[]{:S(2)}) %collective-permute-start.23) | collective-permute-done | bytes 102432 | tf_op jit(solution)/shard_map/ppermute | solution.py:264
  187.6 0.8 collective-permute-done.24.refs_7_
  188.5 1.6 shard_map.88
  (78 shorter events, 1.9 us)
Async XLA Ops:
  6.5 41.7 %all-gather.11.cloned.1.call-start = ((), (), s32[]{:S(2)}) async-start(), calls=%async_computation.2 | async-start | bytes 1437696 | tf_op jit(solution)/shard_map/all_gather | solution.py:282
  8.2 83.3 %all-gather.7.cloned.1.call-start = ((), (), s32[]{:S(2)}) async-start(), calls=%async_computation | async-start | bytes 2764800 | tf_op jit(solution)/shard_map/all_gather | solution.py:291
  8.3 7.2 %collective-permute-start = (bf16[100,384]{1,0:T(8,128)(2,1)}, bf16[100,384]{1,0:T(8,128)(2,1)S(1)}, u32[]{:S(2)}, u32[]{:S(2)}) collective-permute-start(bf16[100,384]{1,0:T(8,128)(2,1)} %bitcast.76), channel_id=1, source_target_pairs={{0,0},{4,32},{8,64},{12,96},{16,128},{20,160},{24,192},{28,224},{3... | collective-permute-start | bytes 230408 | tf_op jit(solution)/shard_map/ppermute | solution.py:285
  15.5 6.1 %collective-permute-start.1 = (bf16[100,768]{1,0:T(8,128)(2,1)S(1)}, bf16[100,768]{1,0:T(8,128)(2,1)S(1)}, u32[]{:S(2)}, u32[]{:S(2)}) collective-permute-start(bf16[100,768]{1,0:T(8,128)(2,1)S(1)} %pad_maximum_fusion.5), channel_id=1, source_target_pairs={{0,1},{1,2},{2,3},{3,0},{4,5},{5,6},{6,7},{7,4},{8,9},{9,10},{10,1... | collective-permute-start | bytes 460808 | tf_op jit(solution)/shard_map/ppermute | solution.py:264
  17.1 6.8 %collective-permute-start.2 = (bf16[100,768]{1,0:T(8,128)(2,1)S(1)}, bf16[100,768]{1,0:T(8,128)(2,1)S(1)}, u32[]{:S(2)}, u32[]{:S(2)}) collective-permute-start(bf16[100,768]{1,0:T(8,128)(2,1)S(1)} %pad_maximum_fusion.5), channel_id=1, source_target_pairs={{0,3},{1,0},{2,1},{3,2},{4,7},{5,4},{6,5},{7,6},{8,11},{9,8},{10,9... | collective-permute-start | bytes 460808 | tf_op jit(solution)/shard_map/ppermute | solution.py:264
  18.5 7.1 %collective-permute-start.3 = (bf16[100,768]{1,0:T(8,128)(2,1)S(1)}, bf16[100,768]{1,0:T(8,128)(2,1)S(1)}, u32[]{:S(2)}, u32[]{:S(2)}) collective-permute-start(bf16[100,768]{1,0:T(8,128)(2,1)S(1)} %pad_maximum_fusion.5), channel_id=1, source_target_pairs={{0,2},{1,3},{2,0},{3,1},{4,6},{5,7},{6,4},{7,5},{8,10},{9,11},{10,... | collective-permute-start | bytes 460808 | tf_op jit(solution)/shard_map/ppermute | solution.py:264
  26.7 128.9 %all-gather.9.cloned.1.call-start = ((), (), s32[]{:S(2)}) async-start(), calls=%async_computation.1 | async-start | bytes 2764800 | tf_op jit(solution)/shard_map/all_gather | solution.py:299
  26.8 2.5 %copy-start.15 = (f32[3200]{0:T(1024)S(1)}, f32[3200]{0:T(1024)}, u32[]{:S(2)}) copy-start(f32[3200]{0:T(1024)} %param.10) | copy-start | bytes 38404
  26.8 2.5 %copy-start.17 = (s32[8]{0:T(128)S(1)}, s32[8]{0:T(128)}, u32[]{:S(2)}) copy-start(s32[8]{0:T(128)} %constant.113.clone) | copy-start | bytes 100
  30.0 2.9 %copy-start.4 = (bf16[1,1024,3200]{2,1,0:T(8,128)(2,1)S(1)}, bf16[1,1024,3200]{2,1,0:T(8,128)(2,1)}, u32[]{:S(2)}) copy-start(bf16[1,1024,3200]{2,1,0:T(8,128)(2,1)} %param.8) | copy-start | bytes 19660804
  40.1 3.0 %copy-start = (bf16[4,1024,800]{2,1,0:T(8,128)(2,1)}, bf16[4,1024,800]{2,1,0:T(8,128)(2,1)S(1)}, u32[]{:S(2)}) copy-start(bf16[4,1024,800]{2,1,0:T(8,128)(2,1)S(1)} %get-tuple-element.18.x_ref) | copy-start | bytes 19660804
  43.1 2.7 %copy-start.5 = (bf16[1024,3200]{1,0:T(8,128)(2,1)}, bf16[1024,3200]{1,0:T(8,128)(2,1)S(1)}, u32[]{:S(2)}) copy-start(bf16[1024,3200]{1,0:T(8,128)(2,1)S(1)} %get-tuple-element.21.normed) | copy-start | bytes 19660804
  49.7 25.4 %copy-start.11 = (bf16[400,768]{1,0:T(8,128)(2,1)}, bf16[400,768]{1,0:T(8,128)(2,1)S(1)}, u32[]{:S(2)}) copy-start(bf16[400,768]{1,0:T(8,128)(2,1)S(1)} %reshape.35.own_top) | copy-start | bytes 1843204
  49.9 25.3 %copy-start.12 = (bf16[400,768]{1,0:T(8,128)(2,1)}, bf16[400,768]{1,0:T(8,128)(2,1)S(1)}, u32[]{:S(2)}) copy-start(bf16[400,768]{1,0:T(8,128)(2,1)S(1)} %reshape.36.own_low) | copy-start | bytes 1843204
  49.9 12.0 %collective-permute-start.4 = (bf16[400,768]{1,0:T(8,128)(2,1)S(1)}, bf16[400,768]{1,0:T(8,128)(2,1)S(1)}, u32[]{:S(2)}, u32[]{:S(2)}) collective-permute-start(bf16[400,768]{1,0:T(8,128)(2,1)S(1)} %reshape.35.own_top), channel_id=1, source_target_pairs={{0,1},{1,2},{2,3},{3,0},{4,5},{5,6},{6,7},{7,4},{8,9},{9,10},{10,1... | collective-permute-start | bytes 1843208 | tf_op jit(solution)/shard_map/ppermute | solution.py:264
  51.2 10.9 %collective-permute-start.7 = (bf16[400,768]{1,0:T(8,128)(2,1)S(1)}, bf16[400,768]{1,0:T(8,128)(2,1)S(1)}, u32[]{:S(2)}, u32[]{:S(2)}) collective-permute-start(bf16[400,768]{1,0:T(8,128)(2,1)S(1)} %reshape.36.own_low), channel_id=1, source_target_pairs={{0,3},{1,0},{2,1},{3,2},{4,7},{5,4},{6,5},{7,6},{8,11},{9,8},{10,9... | collective-permute-start | bytes 1843208 | tf_op jit(solution)/shard_map/ppermute | solution.py:264
  52.6 22.5 %collective-permute-start.5 = (bf16[400,768]{1,0:T(8,128)(2,1)S(1)}, bf16[400,768]{1,0:T(8,128)(2,1)}, u32[]{:S(2)}, u32[]{:S(2)}) collective-permute-start(bf16[400,768]{1,0:T(8,128)(2,1)S(1)} %reshape.36.own_low), channel_id=1, source_target_pairs={{0,1},{1,2},{2,3},{3,0},{4,5},{5,6},{6,7},{7,4},{8,9},{9,10},{10,1... | collective-permute-start | bytes 1843208 | tf_op jit(solution)/shard_map/ppermute | solution.py:264
  52.7 22.4 %collective-permute-start.6 = (bf16[400,768]{1,0:T(8,128)(2,1)S(1)}, bf16[400,768]{1,0:T(8,128)(2,1)}, u32[]{:S(2)}, u32[]{:S(2)}) collective-permute-start(bf16[400,768]{1,0:T(8,128)(2,1)S(1)} %reshape.35.own_top), channel_id=1, source_target_pairs={{0,3},{1,0},{2,1},{3,2},{4,7},{5,4},{6,5},{7,6},{8,11},{9,8},{10,9... | collective-permute-start | bytes 1843208 | tf_op jit(solution)/shard_map/ppermute | solution.py:264
  61.9 13.3 %copy-start.13 = (bf16[400,768]{1,0:T(8,128)(2,1)}, bf16[400,768]{1,0:T(8,128)(2,1)S(1)}, u32[]{:S(2)}) copy-start(bf16[400,768]{1,0:T(8,128)(2,1)S(1)} %collective-permute-done.4.back_top) | copy-start | bytes 1843204
  61.9 26.4 %collective-permute-start.8 = (bf16[400,768]{1,0:T(8,128)(2,1)S(1)}, bf16[400,768]{1,0:T(8,128)(2,1)}, u32[]{:S(2)}, u32[]{:S(2)}) collective-permute-start(bf16[400,768]{1,0:T(8,128)(2,1)S(1)} %collective-permute-done.4.back_top), channel_id=1, source_target_pairs={{0,1},{1,2},{2,3},{3,0},{4,5},{5,6},{6,7},{7,4},{8,9},{9,10},{10,1... | collective-permute-start | bytes 1843208 | tf_op jit(solution)/shard_map/ppermute | solution.py:264
  62.1 13.1 %copy-start.14 = (bf16[400,768]{1,0:T(8,128)(2,1)}, bf16[400,768]{1,0:T(8,128)(2,1)S(1)}, u32[]{:S(2)}) copy-start(bf16[400,768]{1,0:T(8,128)(2,1)S(1)} %collective-permute-done.7.ahead_low) | copy-start | bytes 1843204
  62.1 26.2 %collective-permute-start.9 = (bf16[400,768]{1,0:T(8,128)(2,1)S(1)}, bf16[400,768]{1,0:T(8,128)(2,1)}, u32[]{:S(2)}, u32[]{:S(2)}) collective-permute-start(bf16[400,768]{1,0:T(8,128)(2,1)S(1)} %collective-permute-done.7.ahead_low), channel_id=1, source_target_pairs={{0,3},{1,0},{2,1},{3,2},{4,7},{5,4},{6,5},{7,6},{8,11},{9,8},{10,9... | collective-permute-start | bytes 1843208 | tf_op jit(solution)/shard_map/ppermute | solution.py:264
  107.6 18.2 %collective-permute-start.10 = (bf16[384,512]{1,0:T(8,128)(2,1)}, bf16[384,512]{1,0:T(8,128)(2,1)S(1)}, u32[]{:S(2)}, u32[]{:S(2)}) collective-permute-start(bf16[384,512]{1,0:T(8,128)(2,1)} %get-tuple-element.24.own_ctx), channel_id=1, source_target_pairs={{0,8},{4,12},{8,16},{12,20},{16,24},{20,28},{24,0},{28,4},{1,9},{5... | collective-permute-start | bytes 1179656 | tf_op jit(solution)/shard_map/ppermute | solution.py:264
  108.7 17.2 %collective-permute-start.12 = (bf16[384,512]{1,0:T(8,128)(2,1)}, bf16[384,512]{1,0:T(8,128)(2,1)S(1)}, u32[]{:S(2)}, u32[]{:S(2)}) collective-permute-start(bf16[384,512]{1,0:T(8,128)(2,1)} %get-tuple-element.24.own_ctx), channel_id=1, source_target_pairs={{0,24},{4,28},{8,0},{12,4},{16,8},{20,12},{24,16},{28,20},{1,25},{... | collective-permute-start | bytes 1179656 | tf_op jit(solution)/shard_map/ppermute | solution.py:264
  118.0 1.4 copy-start.1
  119.4 1.1 copy-start.9
  126.0 14.8 %copy-start.6 = (bf16[384,512]{1,0:T(8,128)(2,1)S(1)}, bf16[384,512]{1,0:T(8,128)(2,1)}, u32[]{:S(2)}) copy-start(bf16[384,512]{1,0:T(8,128)(2,1)} %get-tuple-element.24.own_ctx) | copy-start | bytes 1179652
  126.0 13.9 %collective-permute-start.11 = (bf16[576,512]{1,0:T(8,128)(2,1)S(1)}, bf16[576,512]{1,0:T(8,128)(2,1)S(1)}, u32[]{:S(2)}, u32[]{:S(2)}) collective-permute-start(bf16[576,512]{1,0:T(8,128)(2,1)S(1)} %get-tuple-element.50), channel_id=1, source_target_pairs={{0,8},{4,12},{8,16},{12,20},{16,24},{20,28},{24,0},{28,4},{1,9},{5... | collective-permute-start | bytes 1769480 | tf_op jit(solution)/shard_map/ppermute | solution.py:264
  126.7 13.3 %collective-permute-start.13 = (bf16[576,512]{1,0:T(8,128)(2,1)S(1)}, bf16[576,512]{1,0:T(8,128)(2,1)S(1)}, u32[]{:S(2)}, u32[]{:S(2)}) collective-permute-start(bf16[576,512]{1,0:T(8,128)(2,1)S(1)} %get-tuple-element.49), channel_id=1, source_target_pairs={{0,24},{4,28},{8,0},{12,4},{16,8},{20,12},{24,16},{28,20},{1,25},{... | collective-permute-start | bytes 1769480 | tf_op jit(solution)/shard_map/ppermute | solution.py:264
  142.1 13.5 %collective-permute-start.18 = (bf16[4,384,512]{2,1,0:T(8,128)(2,1)}, bf16[4,384,512]{2,1,0:T(8,128)(2,1)}, u32[]{:S(2)}, u32[]{:S(2)}) collective-permute-start(bf16[4,384,512]{2,1,0:T(8,128)(2,1)} %pad_maximum_fusion.1), channel_id=1, source_target_pairs={{0,4},{4,0},{8,12},{12,8},{16,20},{20,16},{24,28},{28,24},{1,5},{5... | collective-permute-start | bytes 4718600 | tf_op jit(solution)/shard_map/ppermute | solution.py:326
  145.3 7.7 %collective-permute-start.14 = (bf16[192,512]{1,0:T(8,128)(2,1)S(1)}, bf16[192,512]{1,0:T(8,128)(2,1)S(1)}, u32[]{:S(2)}, u32[]{:S(2)}) collective-permute-start(bf16[192,512]{1,0:T(8,128)(2,1)S(1)} %get-tuple-element.32), channel_id=1, source_target_pairs={{0,8},{4,12},{8,16},{12,20},{16,24},{20,28},{24,0},{28,4},{1,9},{5... | collective-permute-start | bytes 589832 | tf_op jit(solution)/shard_map/ppermute | solution.py:264
  145.8 7.3 %collective-permute-start.15 = (bf16[192,512]{1,0:T(8,128)(2,1)S(1)}, bf16[192,512]{1,0:T(8,128)(2,1)S(1)}, u32[]{:S(2)}, u32[]{:S(2)}) collective-permute-start(bf16[192,512]{1,0:T(8,128)(2,1)S(1)} %get-tuple-element.34), channel_id=1, source_target_pairs={{0,24},{4,28},{8,0},{12,4},{16,8},{20,12},{24,16},{28,20},{1,25},{... | collective-permute-start | bytes 589832 | tf_op jit(solution)/shard_map/ppermute | solution.py:264
  153.1 2.2 %copy-start.16 = (f32[400]{0:T(512)S(1)}, f32[400]{0:T(512)}, u32[]{:S(2)}) copy-start(f32[400]{0:T(512)} %param.13) | copy-start | bytes 4804
  154.5 15.9 %collective-permute-start.16 = (bf16[4,384,512]{2,1,0:T(8,128)(2,1)}, bf16[4,384,512]{2,1,0:T(8,128)(2,1)}, u32[]{:S(2)}, u32[]{:S(2)}) collective-permute-start(bf16[4,384,512]{2,1,0:T(8,128)(2,1)} %pad_maximum_fusion), channel_id=1, source_target_pairs={{0,4},{4,0},{8,12},{12,8},{16,20},{20,16},{24,28},{28,24},{1,5},{5... | collective-permute-start | bytes 4718600 | tf_op jit(solution)/shard_map/ppermute | solution.py:326
  155.6 1.7 copy-start.2
  157.3 1.0 copy-start.8
  158.3 12.0 %copy-start.3 = (bf16[3200,384]{1,0:T(8,128)(2,1)S(1)}, bf16[3200,384]{1,0:T(8,128)(2,1)}, u32[]{:S(2)}) copy-start(bf16[3200,384]{1,0:T(8,128)(2,1)} %all-gather.9.cloned.1.call-done) | copy-start | bytes 7372804
  158.3 12.0 %copy-start.7 = (bf16[384,512]{1,0:T(8,128)(2,1)S(1)}, bf16[384,512]{1,0:T(8,128)(2,1)}, u32[]{:S(2)}) copy-start(bf16[384,512]{1,0:T(8,128)(2,1)} %get-tuple-element.38.ahead) | copy-start | bytes 1179652
  162.8 13.2 %collective-permute-start.19 = (bf16[400,128]{1,0:T(8,128)(2,1)S(1)}, bf16[400,128]{1,0:T(8,128)(2,1)S(1)}, u32[]{:S(2)}, u32[]{:S(2)}) collective-permute-start(bf16[400,128]{1,0:T(8,128)(2,1)S(1)} %get-tuple-element.46), channel_id=1, source_target_pairs={{0,64},{32,96},{64,128},{96,160},{128,192},{160,224},{192,0},{224,... | collective-permute-start | bytes 307208 | tf_op jit(solution)/shard_map/ppermute | solution.py:264
  162.9 17.2 %collective-permute-start.20 = (bf16[400,128]{1,0:T(8,128)(2,1)S(1)}, bf16[400,128]{1,0:T(8,128)(2,1)S(1)}, u32[]{:S(2)}, u32[]{:S(2)}) collective-permute-start(bf16[400,128]{1,0:T(8,128)(2,1)S(1)} %get-tuple-element.45), channel_id=1, source_target_pairs={{0,96},{32,128},{64,160},{96,192},{128,224},{160,0},{192,32},{224,... | collective-permute-start | bytes 307208 | tf_op jit(solution)/shard_map/ppermute | solution.py:264
  167.0 13.2 %collective-permute-start.21 = (bf16[400,128]{1,0:T(8,128)(2,1)S(1)}, bf16[400,128]{1,0:T(8,128)(2,1)S(1)}, u32[]{:S(2)}, u32[]{:S(2)}) collective-permute-start(bf16[400,128]{1,0:T(8,128)(2,1)S(1)} %get-tuple-element.44), channel_id=1, source_target_pairs={{0,128},{32,160},{64,192},{96,224},{128,0},{160,32},{192,64},{224,... | collective-permute-start | bytes 307208 | tf_op jit(solution)/shard_map/ppermute | solution.py:264
  169.6 12.5 %collective-permute-start.22 = (bf16[400,128]{1,0:T(8,128)(2,1)S(1)}, bf16[400,128]{1,0:T(8,128)(2,1)S(1)}, u32[]{:S(2)}, u32[]{:S(2)}) collective-permute-start(bf16[400,128]{1,0:T(8,128)(2,1)S(1)} %get-tuple-element.43), channel_id=1, source_target_pairs={{0,160},{32,192},{64,224},{96,0},{128,32},{160,64},{192,96},{224,1... | collective-permute-start | bytes 307208 | tf_op jit(solution)/shard_map/ppermute | solution.py:264
  170.3 18.1 %copy-start.10 = (s32[4,8]{1,0:T(4,128)S(1)}, s32[4,8]{1,0:T(4,128)}, u32[]{:S(2)}) copy-start(s32[4,8]{1,0:T(4,128)} %order_ref.1) | copy-start | bytes 388
  174.7 10.6 %collective-permute-start.17 = (bf16[400,128]{1,0:T(8,128)(2,1)S(1)}, bf16[400,128]{1,0:T(8,128)(2,1)S(1)}, u32[]{:S(2)}, u32[]{:S(2)}) collective-permute-start(bf16[400,128]{1,0:T(8,128)(2,1)S(1)} %get-tuple-element.41), channel_id=1, source_target_pairs={{0,32},{32,64},{64,96},{96,128},{128,160},{160,192},{192,224},{224... | collective-permute-start | bytes 307208 | tf_op jit(solution)/shard_map/ppermute | solution.py:264
  176.0 11.6 %collective-permute-start.23 = (bf16[400,128]{1,0:T(8,128)(2,1)S(1)}, bf16[400,128]{1,0:T(8,128)(2,1)S(1)}, u32[]{:S(2)}, u32[]{:S(2)}) collective-permute-start(bf16[400,128]{1,0:T(8,128)(2,1)S(1)} %get-tuple-element.40), channel_id=1, source_target_pairs={{0,192},{32,224},{64,0},{96,32},{128,64},{160,96},{192,128},{224,1... | collective-permute-start | bytes 307208 | tf_op jit(solution)/shard_map/ppermute | solution.py:264
  180.2 8.3 %collective-permute-start.24 = (bf16[400,128]{1,0:T(8,128)(2,1)S(1)}, bf16[400,128]{1,0:T(8,128)(2,1)S(1)}, u32[]{:S(2)}, u32[]{:S(2)}) collective-permute-start(bf16[400,128]{1,0:T(8,128)(2,1)S(1)} %get-tuple-element.39), channel_id=1, source_target_pairs={{0,224},{32,0},{64,32},{96,64},{128,96},{160,128},{192,160},{224,1... | collective-permute-start | bytes 307208 | tf_op jit(solution)/shard_map/ppermute | solution.py:264
Sparse Core Ops, SparseCore 0:
  9.1 39.0 all-gather.10
  50.0 41.4 all-gather.6
  93.3 40.5 all-gather.8
where the time goes:
time: 197 us
  waiting for transfers between devices  57.6 us (29%)
  Pallas kernels  49.2 us (25%)
  starting transfers between devices  48.5 us (25%)
  local copies, waits for them, and re-layouts  22.6 us (11%)
  between operations  14.2 us (7%)
  other arithmetic  4.58 us (2%)
    ppermute x22, waiting for transfers between devices, around(): return lax.ppermute(x, axis, [(i, (i + step) % size) for i in range(size)])  49.5 us
    ppermute x22, starting transfers between devices, around(): return lax.ppermute(x, axis, [(i, (i + step) % size) for i in range(size)])  39.5 us
    pallas_call x1, Pallas kernels, late(): pl.pallas_call(late_body, grid_spec=pltpu.PrefetchScalarGridSpec(num_scal...  16.1 us
    unnamed x37, local copies, waits for them, and re-layouts  13.9 us
    pallas_call x1, Pallas kernels, early(): pl.pallas_call(early_body, grid_spec=pltpu.PrefetchScalarGridSpec(num_sca...  10.3 us
    pallas_call x2, Pallas kernels, project(): pl.pallas_call(functools.partial(project_body, first), in_specs=[pl.Block...  8.81 us
    pallas_call x1, Pallas kernels, normalise(): pl.pallas_call(norm_body, grid=(rows // tile,), in_specs=[pl.BlockSpec((t...  7.21 us
    pallas_call x1, Pallas kernels, attend(): pl.pallas_call(attend_body, grid_spec=pltpu.PrefetchScalarGridSpec(num_sc...  5.13 us
  transfers between devices with their start and end apart: 28, of which 17 were waited for; matrix products, arithmetic and copies ran while one was open for 6% of the time, Pallas kernels for 24%

commit v1 on v0

--- a/solution.py
+++ b/solution.py
@@ -12,7 +12,6 @@
 BF = jnp.bfloat16
 F32 = jnp.float32
 ORDER = (4, 3, 5, 2, 6, 1, 7, 0)
-GROUPS = ((0, 4), (4, 8))
 
 
 def norm_body(x_ref, gain_ref, plain, by_dp):
@@ -48,36 +47,43 @@
     )(x, gain[None])
 
 
-def early_body(at_ref, x_ref, own_top, own_low, back_top, back_low, ahead_top, ahead_low, out_ref):
-    total = jnp.zeros(out_ref.shape, F32)
-    for k, (top, low) in enumerate(((own_top, own_low), (back_top, back_low), (ahead_top, ahead_low))):
-        total += jnp.dot(x_ref[at_ref[k], :, :400], top[...], preferred_element_type=F32)
-        total += jnp.dot(x_ref[at_ref[k], :, 400:], low[...], preferred_element_type=F32)
+def early_body(at_ref, *refs):
+    pairs = (len(refs) - 1) // 3
+    sums, halves, out_ref = refs[: len(refs) - 1 - 3 * pairs], refs[-1 - 2 * pairs : -1], refs[-1]
+    blocks = refs[len(sums) : len(sums) + pairs]
+    total = sums[0][...] if sums else None
+    for k in range(pairs):
+        term = jnp.dot(blocks[k][0, :, :400], halves[2 * k][...], preferred_element_type=F32)
+        total = term if total is None else total + term
+        total += jnp.dot(blocks[k][0, :, 400:], halves[2 * k + 1][...], preferred_element_type=F32)
     out_ref[...] = total
 
 
-def early(at, by_dp, *halves):
+def early(at, by_dp, sums, *halves):
     rows, deep = by_dp.shape[1:]
     wide = halves[0].shape[1]
-    tile = 256
-    half = pl.BlockSpec((deep // 2, wide), lambda r, a: (0, 0))
+    pairs = len(halves) // 2
+    tile = rows // 4
+    part = pl.BlockSpec((tile, wide), lambda r, a: (r, 0))
+    blocks = [
+        pl.BlockSpec((1, tile, deep), lambda r, a, k=k: (a[k], r, 0)) for k in range(pairs)
+    ]
     return pl.pallas_call(
         early_body,
         grid_spec=pltpu.PrefetchScalarGridSpec(
             num_scalar_prefetch=1,
             grid=(rows // tile,),
-            in_specs=[
-                pl.BlockSpec((4, tile, deep), lambda r, a: (0, r, 0)),
-            ]
-            + [half] * 6,
-            out_specs=pl.BlockSpec((tile, wide), lambda r, a: (r, 0)),
+            in_specs=[part] * len(sums)
+            + blocks
+            + [pl.BlockSpec((deep // 2, wide), lambda r, a: (0, 0))] * len(halves),
+            out_specs=part,
         ),
         out_shape=jax.ShapeDtypeStruct((rows, wide), F32),
-        compiler_params=pltpu.CompilerParams(vmem_limit_bytes=58 * 2**20),
+        compiler_params=pltpu.CompilerParams(vmem_limit_bytes=54 * 2**20),
         cost_estimate=pl.CostEstimate(
-            flops=6 * rows * deep * wide, bytes_accessed=15_000_000, transcendentals=0
-        ),
-    )(at, by_dp, *halves)
+            flops=2 * pairs * rows * deep * wide, bytes_accessed=10_000_000, transcendentals=0
+        ),
+    )(at, *sums, *[by_dp] * pairs, *halves)
 
 
 def attend_tile(live_keys, query, key, vt, out_ref):
@@ -199,43 +205,75 @@
     )(info, qk, qk, qk, vt)
 
 
-def project_body(first, info_ref, own_ctx, back, ahead, far, sibling, w_hbm, own_ref, scale_ref, out_ref, w, sems):
-    copies = [
-        pltpu.make_async_copy(w_hbm.at[info_ref[j]], w.at[j], sems.at[j]) for j in range(8)
-    ]
+def project_body(cuts, info_ref, *refs):
+    sources, (w_hbm, mine_ref, theirs_ref, ctx, w, sems) = refs[:5], refs[5:]
+    pairs = []
+    for src, (first, slot, at, rows) in zip(sources, cuts):
+        pairs.append((src.at[pl.ds(first, rows)], ctx.at[slot, pl.ds(at, rows)]))
+    pairs += [(w_hbm.at[info_ref[j]], w.at[j]) for j in (4, 5, 6, 7, 0, 1, 2, 3)]
+    copies = [pltpu.make_async_copy(*pair, sems.at[i]) for i, pair in enumerate(pairs)]
     for copy in copies:
         copy.start()
-    near = (own_ctx, back, ahead, far)
+    needs = ((0,), (1,), (2,), (3, 4))
     total = None
-    for j in range(8):
-        copies[j].wait()
-        ctx = near[j][...] if j < 4 else sibling[j - 4]
-        term = jnp.dot(w[j], ctx, preferred_element_type=F32)
+    for j in range(4):
+        for i in needs[j] + (5 + j,):
+            copies[i].wait()
+        term = jnp.dot(w[4 + j], ctx[j], preferred_element_type=F32)
         total = term if total is None else total + term
-    total = scale_ref[...] * total
-    for c in range(out_ref.shape[0]):
-        row = lax.broadcasted_iota(jnp.int32, (1, 128), 1) + info_ref[9 + c]
-        value = own_ref[first + c].astype(F32) + total[:, c * 128 : c * 128 + 128]
-        out_ref[c] = jnp.where(row < info_ref[8], value, 0.0).astype(BF)
-
-
-def project(first, info, near, sibling, w8, own, scale):
+    theirs_ref[...] = total.astype(BF)
+    total = None
+    for j in range(4):
+        copies[9 + j].wait()
+        term = jnp.dot(w[j], ctx[j], preferred_element_type=F32)
+        total = term if total is None else total + term
+    mine_ref[...] = total
+
+
+def project(info, parts, w8):
+    tall, deep = w8.shape[1:]
+    columns = parts[0][0].shape[1]
+    whole = pl.BlockSpec(memory_space=pltpu.VMEM)
+    return pl.pallas_call(
+        functools.partial(project_body, [part[1:] for part in parts]),
+        in_specs=[pl.BlockSpec(memory_space=pltpu.SMEM)] + [pl.BlockSpec(memory_space=pl.ANY)] * 6,
+        out_specs=[whole, whole],
+        out_shape=[
+            jax.ShapeDtypeStruct((tall, columns), F32),
+            jax.ShapeDtypeStruct((tall, columns), BF),
+        ],
+        scratch_shapes=[
+            pltpu.VMEM((4, deep, columns), BF),
+            pltpu.VMEM(w8.shape, BF),
+            pltpu.SemaphoreType.DMA((13,)),
+        ],
+        compiler_params=pltpu.CompilerParams(vmem_limit_bytes=50 * 2**20),
+        cost_estimate=pl.CostEstimate(
+            flops=2 * columns * tall * deep * 8, bytes_accessed=6_000_000, transcendentals=0
+        ),
+    )(info, *[part[0] for part in parts], w8)
+
+
+def finish_body(first, info_ref, mine_ref, theirs_ref, own_ref, scale_ref, *out_refs):
+    for c, out_ref in enumerate(out_refs):
+        at = slice(c * 128, c * 128 + 128)
+        total = scale_ref[...] * (mine_ref[:, at] + theirs_ref[:, at].astype(F32))
+        row = lax.broadcasted_iota(jnp.int32, (1, 128), 1) + info_ref[1 + c]
+        value = own_ref[first + c].astype(F32) + total
+        out_ref[...] = jnp.where(row < info_ref[0], value, 0.0).astype(BF)
+
+
+def finish(first, info, mine, theirs, own, scale):
     chunks, tall = 4, own.shape[1]
     whole = pl.BlockSpec(memory_space=pltpu.VMEM)
     return pl.pallas_call(
-        functools.partial(project_body, first),
-        in_specs=[pl.BlockSpec(memory_space=pltpu.SMEM)]
-        + [whole] * 5
-        + [pl.BlockSpec(memory_space=pl.ANY)]
-        + [whole] * 2,
-        out_specs=whole,
-        out_shape=jax.ShapeDtypeStruct((chunks, tall, 128), BF),
-        scratch_shapes=[pltpu.VMEM(w8.shape, BF), pltpu.SemaphoreType.DMA((8,))],
-        compiler_params=pltpu.CompilerParams(vmem_limit_bytes=16 * 2**20),
-        cost_estimate=pl.CostEstimate(
-            flops=2 * chunks * tall * 384 * 8 * 128, bytes_accessed=6_000_000, transcendentals=0
-        ),
-    )(info, *near, sibling, w8, own, scale)
+        functools.partial(finish_body, first),
+        in_specs=[pl.BlockSpec(memory_space=pltpu.SMEM)] + [whole] * 4,
+        out_specs=[whole] * chunks,
+        out_shape=[jax.ShapeDtypeStruct((tall, 128), BF)] * chunks,
+        compiler_params=pltpu.CompilerParams(vmem_limit_bytes=24 * 2**20),
+        cost_estimate=pl.CostEstimate(flops=1000, bytes_accessed=1000, transcendentals=0),
+    )(info, mine, theirs, own, scale)
 
 
 def deliver_body(info_ref, order_ref, *refs):
@@ -283,7 +321,14 @@
     own_top, own_low = block_b[:4].reshape(400, 768), block_b[4:].reshape(400, 768)
 
     w_o = lax.ppermute(
-        w_out.T, ("section", "tp"), [(s * 8 + t, t * 8 + s) for s in range(8) for t in range(8)]
+        w_out.T,
+        ("section", "tp"),
+        [
+            (s * 8 + y * 2 + c, (y * 2 + s % 2) * 8 + s // 2 * 2 + c)
+            for s in range(8)
+            for y in range(4)
+            for c in range(2)
+        ],
     )
     w_a = jnp.concatenate([w_qkv[2], w_o], axis=1)
     parts = (w_a, around(w_a, "dp", 1, 4), around(w_a, "dp", -1, 4), around(w_a, "dp", 2, 4))
@@ -292,9 +337,19 @@
     rel = (sec + jnp.array(ORDER, jnp.int32)) % 8
     own = lax.dynamic_slice_in_dim(whole, tp * share, share, 1)
     own = jnp.take(own.reshape(8, 128, share).transpose(0, 2, 1), rel, axis=0, mode="clip")
+    rounds = [(y + off) % 4 * 2 for off in (0, 3, 1, 2)]
+    weights_at = jnp.stack([r + core for r in rounds] + [r + 1 - core for r in rounds]).astype(jnp.int32)
+    scale = jnp.broadcast_to(layer_scale[:, None], (share, 128))
+
+    infos = [jnp.concatenate([counts, rel[first : first + 4] * 128]) for first in (0, 4)]
+    ask = jnp.concatenate([counts, rel[4:]])
+    at = jnp.stack([dp, (dp + 3) % 4, (dp + 1) % 4, (dp + 2) % 4]).astype(jnp.int32)
+    at = jnp.concatenate([at, counts, rel[:4]])
+    at_early = at[:1], at[1:3]
+    place_info = jnp.stack([sec, dp]).astype(jnp.int32)
     normed, by_dp = normalise(whole, norm_gain)
-    own_top, own_low, block_o, normed, by_dp, own = lax.optimization_barrier(
-        (own_top, own_low, block_a[:, 384:], normed, by_dp, own)
+    own_top, own_low, block_o, normed, by_dp, own, scale, infos, ask, at, at_early, place_info, weights_at = lax.optimization_barrier(
+        (own_top, own_low, block_a[:, 384:], normed, by_dp, own, scale, infos, ask, at, at_early, place_info, weights_at)
     )
     w8 = lax.all_gather(block_o, "section", axis=0, tiled=False)
 
@@ -305,48 +360,34 @@
     far_top = around(back_top, "dp", 1, 4)
     far_low = around(ahead_low, "dp", -1, 4)
 
-    at = jnp.stack([dp, (dp + 3) % 4, (dp + 1) % 4, (dp + 2) % 4]).astype(jnp.int32)
-    at = jnp.concatenate([at, counts, rel[:4]])
-    sums = early(at, by_dp, own_top, own_low, back_top, back_low, ahead_top, ahead_low)
+    sums = early(at_early[0], by_dp, (), own_top, own_low)
+    sums = early(at_early[1], by_dp, (sums,), back_top, back_low, ahead_top, ahead_low)
     qk, value_t, ctx0 = late(at, sums, by_dp, far_top, far_low, normed, w_v)
 
-    near_groups = [2 * ((y + off) % 4) + core for off in (0, 3, 1, 2)]
-    far_groups = [2 * ((y + off) % 4) + 1 - core for off in (0, 3, 1, 2)]
-    scale = layer_scale[:, None]
-
     received = {}
-    info = jnp.stack(near_groups + far_groups + [count]).astype(jnp.int32)
-    infos = [jnp.concatenate([info, rel[first:last] * 128]) for first, last in GROUPS]
-    ask = jnp.concatenate([counts, rel[4:]])
-
     def both_ways(up, down):
         return around(up, "tp", 2, 8), around(down, "tp", -2, 8)
 
-    def shared(near):
-        return lax.ppermute(jnp.stack(near), "tp", [(i, i ^ 1) for i in range(8)])
-
-    def sent(encoded, first, last):
-        for j in range(first, last):
-            k = ORDER[j]
-            piece = encoded[j - first]
+    def encoded(half, parts):
+        mine, theirs = project(weights_at, parts, w8)
+        theirs = lax.ppermute(theirs, "tp", [(i, i ^ 1) for i in range(8)])
+        return finish(half * 4, infos[half], mine, theirs, own, scale)
+
+    def sent(half, pieces):
+        for k, piece in zip(ORDER[half * 4 : half * 4 + 4], pieces):
             received[k] = around(piece, "section", k, 8) if k else piece
 
-    back0, ahead0 = both_ways(ctx0, ctx0)
+    back, ahead = both_ways(ctx0, ctx0)
     ctx1 = attend(ask, 512, qk, value_t)
     up, down = both_ways(
-        jnp.concatenate([ctx1, back0[:192]], axis=0), jnp.concatenate([ctx1, ahead0[192:]], axis=0)
+        jnp.concatenate([ctx1, back[:192]], axis=0), jnp.concatenate([ctx1, ahead[192:]], axis=0)
     )
-    near0 = (ctx0, back0, ahead0, jnp.concatenate([up[384:], down[384:]], axis=0))
-    back1, ahead1 = up[:384], down[:384]
-    top, low = both_ways(back1[:192], ahead1[192:])
-    near1 = (ctx1, back1, ahead1, jnp.concatenate([top, low], axis=0))
-    sibling0 = shared(near0)
-    encoded0 = project(0, infos[0], near0, sibling0, w8, own, scale)
-    sent(encoded0, 0, 4)
-    sibling1 = shared(near1)
-    encoded1 = project(4, infos[1], near1, sibling1, w8, own, scale)
-    sent(encoded1, 4, 8)
-    arranged = deliver(jnp.stack([sec, dp]).astype(jnp.int32), order, [received[k] for k in range(8)])
+    top, low = both_ways(up[:192], down[192:384])
+    far = ((up, 384, 3, 0, 192), (down, 384, 3, 192, 192))
+    sent(0, encoded(0, ((ctx0, 0, 0, 0, 384), (back, 0, 1, 0, 384), (ahead, 0, 2, 0, 384)) + far))
+    far = ((top, 0, 3, 0, 192), (low, 0, 3, 192, 192))
+    sent(1, encoded(1, ((ctx1, 0, 0, 0, 384), (up, 0, 1, 0, 384), (down, 0, 2, 0, 384)) + far))
+    arranged = deliver(place_info, order, [received[k] for k in range(8)])
     return arranged.transpose(0, 2, 1)[None]
 
 

time: 197 us -> 195 us (0.990)
  waiting for transfers between devices: 57.6 us -> 50.1 us
  Pallas kernels: 49.2 us -> 55.6 us
  other arithmetic: 4.58 us -> 1.63 us
    ppermute x22, waiting for transfers between devices: 49.5 us -> 42.1 us  [around(): return lax.ppermute(x, axis, [(i, (i + step) % size) for i in range(size)])]
    pallas_call x1 -> x2, Pallas kernels: 10.3 us -> 14.3 us  [early(): pl.pallas_call(early_body, grid_spec=pltpu.PrefetchScalarGridSpec(num_sca...]
    another operation x4 -> x1, other arithmetic: 3.62 us -> 0.59 us  [shards(): jnp.stack([dp, (dp + 3) % 4, (dp + 1) % 4, (dp + 2) % 4]).astype(jnp.int32)]
    ppermute x22, starting transfers between devices: 39.5 us -> 42.4 us  [around(): return lax.ppermute(x, axis, [(i, (i + step) % size) for i in range(size)])]
    all_gather x1, waiting for transfers between devices: 2.46 us -> 5.34 us  [shards(): block_b = lax.all_gather(w_b, 'section', axis=0, tiled=False)]
    ppermute x3, starting transfers between devices: 8.88 us -> 6.2 us  [the longest x2 4.65 us: encoded(): theirs = lax.ppermute(theirs, 'tp', [(i, i ^ 1) for i in range(8)])]
    pallas_call x2 -> x4, Pallas kernels: 8.81 us -> 11.3 us  [the longest x2 9.77 us: project(): pl.pallas_call(functools.partial(project_body, [part[1:] for part in part...]
    ppermute x3, waiting for transfers between devices: 2.3 us -> 0.01 us  [the longest x2 0.01 us: encoded(): theirs = lax.ppermute(theirs, 'tp', [(i, i ^ 1) for i in range(8)])]
  transfers between devices with their start and end apart: 28 -> 28, of which waited for: 17 -> 14; matrix products, arithmetic and copies ran while one was open for 6% -> 5% of each run, Pallas kernels for 24% -> 28%
where the time goes in v1:
time: 195 us; the launch traced here: 193 us
  Pallas kernels  55.6 us (29%)
  waiting for transfers between devices  50.1 us (26%)
  starting transfers between devices  48.7 us (25%)
  local copies, waits for them, and re-layouts  22.8 us (12%)
  between operations  14.2 us (7%)
    ppermute x22, starting transfers between devices, around(): return lax.ppermute(x, axis, [(i, (i + step) % size) for i in range(size)])  42.4 us
    ppermute x22, waiting for transfers between devices, around(): return lax.ppermute(x, axis, [(i, (i + step) % size) for i in range(size)])  42.1 us
    pallas_call x1, Pallas kernels, late(): pl.pallas_call(late_body, grid_spec=pltpu.PrefetchScalarGridSpec(num_scal...  16.2 us
    pallas_call x2, Pallas kernels, early(): pl.pallas_call(early_body, grid_spec=pltpu.PrefetchScalarGridSpec(num_sca...  14.3 us
    unnamed x36, local copies, waits for them, and re-layouts  13.8 us
    pallas_call x2, Pallas kernels, project(): pl.pallas_call(functools.partial(project_body, [part[1:] for part in part...  9.77 us
    pallas_call x1, Pallas kernels, normalise(): pl.pallas_call(norm_body, grid=(rows // tile,), in_specs=[pl.BlockSpec((t...  7.23 us
    all_gather x1, waiting for transfers between devices, shards(): block_b = lax.all_gather(w_b, 'section', axis=0, tiled=False)  5.34 us
  transfers between devices with their start and end apart: 28, of which 14 were waited for; matrix products, arithmetic and copies ran while one was open for 5% of the time, Pallas kernels for 28%

profile of v1, /device:TPU:1, one launch (start us, length us, event | category | flops | bytes accessed | tf_op | source)
XLA Modules:
  0.0 193.0 jit_solution(3081859067684300842)
XLA Ops:
  6.5 1.0 slice_bitcast_fusion
  7.5 0.7 maximum_bitcast_fusion
  8.3 1.5 collective-permute-start
  9.9 2.1 %collective-permute-start.1 = (bf16[100,768]{1,0:T(8,128)(2,1)S(1)}, bf16[100,768]{1,0:T(8,128)(2,1)S(1)}, u32[]{:S(2)}, u32[]{:S(2)}) collective-permute-start(bf16[100,768]{1,0:T(8,128)(2,1)S(1)} %pad_maximum_fusion.2), channel_id=1, source_target_pairs={{0,1},{1,2},{2,3},{3,0},{4,5},{5,6},{6,7},{7,4},{8,9},{9,10},{10,1... | collective-permute-start | bytes 460808 | tf_op jit(solution)/shard_map/ppermute | solution.py:302
  12.0 1.4 collective-permute-start.2
  13.4 1.6 collective-permute-start.3
  15.0 0.9 collective-permute-done.1
  15.9 0.2 collective-permute-done.2
  16.1 4.5 %collective-permute-done.3 = bf16[100,768]{1,0:T(8,128)(2,1)S(1)} collective-permute-done((bf16[100,768]{1,0:T(8,128)(2,1)S(1)}, bf16[100,768]{1,0:T(8,128)(2,1)S(1)}, u32[]{:S(2)}, u32[]{:S(2)}) %collective-permute-start.3) | collective-permute-done | bytes 153632 | tf_op jit(solution)/shard_map/ppermute | solution.py:302
  20.8 0.9 fusion.2
  22.5 1.8 constant_dynamic-slice_fusion
  24.3 0.6 copy.12
  25.0 0.7 gather_fusion
  25.8 0.6 concatenate.31.at_ref
  26.5 2.9 %copy-done.2 = bf16[1,1024,3200]{2,1,0:T(8,128)(2,1)S(1)} copy-done((bf16[1,1024,3200]{2,1,0:T(8,128)(2,1)S(1)}, bf16[1,1024,3200]{2,1,0:T(8,128)(2,1)}, u32[]{:S(2)}) %copy-start.2) | copy-done | bytes 6553624
  29.3 7.2 %shard_map.82 = (bf16[1024,3200]{1,0:T(8,128)(2,1)S(1)}, bf16[4,1024,800]{2,1,0:T(8,128)(2,1)S(1)}) custom-call(bf16[1024,3200]{1,0:T(8,128)(2,1)S(1)} %bitcast.37, f32[1,3200]{1,0:T(1,128)S(1)} %broadcast_in_dim.36.gain_ref), custom_call_target="tpu_custom_call" | custom-call | flops 30000000 | bytes 20000000 | tf_op jit(solution)/shard_map/pallas_call | solution.py:30
  36.6 2.9 %copy-done = bf16[4,1024,800]{2,1,0:T(8,128)(2,1)} copy-done((bf16[4,1024,800]{2,1,0:T(8,128)(2,1)}, bf16[4,1024,800]{2,1,0:T(8,128)(2,1)S(1)}, u32[]{:S(2)}) %copy-start) | copy-done | bytes 6553624
  39.5 2.8 %copy-done.3 = bf16[1024,3200]{1,0:T(8,128)(2,1)} copy-done((bf16[1024,3200]{1,0:T(8,128)(2,1)}, bf16[1024,3200]{1,0:T(8,128)(2,1)S(1)}, u32[]{:S(2)}) %copy-start.3) | copy-done | bytes 6553624
  42.3 0.6 pad_add_fusion.3
  43.0 5.3 %all-gather.11.cloned.1.call-done = bf16[8,100,768]{2,1,0:T(8,128)(2,1)} async-done(((bf16[1,100,768]{2,1,0:T(8,128)(2,1)}), bf16[8,100,768]{2,1,0:T(8,128)(2,1)}) %all-gather.11.cloned.1.call-update) | async-done | bytes 1228816 | tf_op jit(solution)/shard_map/all_gather | solution.py:320
  48.3 1.4 fusion.1
  49.7 0.1 reshape.36.refs_1_
  49.8 0.1 reshape.37.refs_2_
  50.1 1.3 collective-permute-start.4
  51.4 1.5 collective-permute-start.7
  52.9 2.7 %collective-permute-start.6 = (bf16[400,768]{1,0:T(8,128)(2,1)S(1)}, bf16[400,768]{1,0:T(8,128)(2,1)S(1)}, u32[]{:S(2)}, u32[]{:S(2)}) collective-permute-start(bf16[400,768]{1,0:T(8,128)(2,1)S(1)} %reshape.36.refs_1_), channel_id=1, source_target_pairs={{0,3},{1,0},{2,1},{3,2},{4,7},{5,4},{6,5},{7,6},{8,11},{9,8},{10,9... | collective-permute-start | bytes 1843208 | tf_op jit(solution)/shard_map/ppermute | solution.py:302
  55.6 6.7 %collective-permute-done.4.refs_3_ = bf16[400,768]{1,0:T(8,128)(2,1)S(1)} collective-permute-done((bf16[400,768]{1,0:T(8,128)(2,1)S(1)}, bf16[400,768]{1,0:T(8,128)(2,1)S(1)}, u32[]{:S(2)}, u32[]{:S(2)}) %collective-permute-start.4) | collective-permute-done | bytes 614432 | tf_op jit(solution)/shard_map/ppermute | solution.py:302
  62.3 2.7 %collective-permute-start.9 = (bf16[400,768]{1,0:T(8,128)(2,1)S(1)}, bf16[400,768]{1,0:T(8,128)(2,1)S(1)}, u32[]{:S(2)}, u32[]{:S(2)}) collective-permute-start(bf16[400,768]{1,0:T(8,128)(2,1)S(1)} %collective-permute-done.7.refs_6_), channel_id=1, source_target_pairs={{0,3},{1,0},{2,1},{3,2},{4,7},{5,4},{6,5},{7,6},{8,11},{9,8},{10,9... | collective-permute-start | bytes 1843208 | tf_op jit(solution)/shard_map/ppermute | solution.py:302
  65.0 5.5 %shard_map.83.refs_0_ = f32[1024,768]{1,0:T(8,128)} custom-call(s32[1]{0:T(128)} %bitcast.12.at_ref, bf16[4,1024,800]{2,1,0:T(8,128)(2,1)} %copy-done, bf16[400,768]{1,0:T(8,128)(2,1)} %copy-done.7, bf16[400,768]{1,0:T(8,128)(2,1)} %copy-done.8), custom_call_target="tpu_custom_call" | custom-call | flops 1258291200 | bytes 10000000 | tf_op jit(solution)/shard_map/pallas_call | solution.py:71
  70.5 4.9 %collective-permute-done.5.refs_4_ = bf16[400,768]{1,0:T(8,128)(2,1)S(1)} collective-permute-done((bf16[400,768]{1,0:T(8,128)(2,1)S(1)}, bf16[400,768]{1,0:T(8,128)(2,1)S(1)}, u32[]{:S(2)}, u32[]{:S(2)}) %collective-permute-start.5) | collective-permute-done | bytes 614432 | tf_op jit(solution)/shard_map/ppermute | solution.py:302
  75.5 0.8 copy-done.13
  76.3 0.8 copy-done.14
  77.1 8.7 %shard_map.84.sums = f32[1024,768]{1,0:T(8,128)} custom-call(s32[2]{0:T(128)} %get-tuple-element.44.at_ref, f32[1024,768]{1,0:T(8,128)} %shard_map.83.refs_0_, bf16[4,1024,800]{2,1,0:T(8,128)(2,1)} %copy-done, bf16[4,1024,800]{2,1,0:T(8,128)(2,1)} %copy-done, bf16[400,768]{1,0:T(8,128)(2,1)} %copy-done.10, bf16[400,768]{1,0:T(8,128)(2,1)} %copy-done.13, ...), custom_call_target="tpu_custom_call" | custom-call | flops 2516582400 | bytes 10000000 | tf_op jit(solution)/shard_map/pallas_call | solution.py:71
  85.8 2.9 %collective-permute-done.8.top = bf16[400,768]{1,0:T(8,128)(2,1)S(1)} collective-permute-done((bf16[400,768]{1,0:T(8,128)(2,1)S(1)}, bf16[400,768]{1,0:T(8,128)(2,1)S(1)}, u32[]{:S(2)}, u32[]{:S(2)}) %collective-permute-start.8) | collective-permute-done | bytes 614432 | tf_op jit(solution)/shard_map/ppermute | solution.py:302
  88.7 2.6 %all-gather.7.cloned.1.call-done.w_ref = bf16[3200,384]{1,0:T(8,128)(2,1)} async-done(((bf16[400,384]{1,0:T(8,128)(2,1)}), bf16[3200,384]{1,0:T(8,128)(2,1)}) %all-gather.7.cloned.1.call-update) | async-done | bytes 2457616 | tf_op jit(solution)/shard_map/all_gather | solution.py:336
  91.3 16.2 %shard_map.85 = (bf16[1024,768]{1,0:T(8,128)(2,1)}, bf16[384,1024]{1,0:T(8,128)(2,1)}, bf16[384,512]{1,0:T(8,128)(2,1)}) custom-call(s32[9]{0:T(128)} %concatenate.31.at_ref, f32[1024,768]{1,0:T(8,128)} %shard_map.84.sums, bf16[4,1024,800]{2,1,0:T(8,128)(2,1)} %copy-done, bf16[400,768]{1,0:T(8,128)(2,1)} %copy-done.9, bf16[400,768]{1,0:T(8,128)(2,1)} %copy-done.12, ...), custom_call_target="tpu_custom_call" | custom-call | flops 4580179968 | bytes 18000000 | tf_op jit(solution)/shard_map/pallas_call | solution.py:146
  107.5 1.2 collective-permute-start.10
  108.7 7.2 %collective-permute-start.12 = (bf16[384,512]{1,0:T(8,128)(2,1)}, bf16[384,512]{1,0:T(8,128)(2,1)S(1)}, u32[]{:S(2)}, u32[]{:S(2)}) collective-permute-start(bf16[384,512]{1,0:T(8,128)(2,1)} %get-tuple-element.52.refs_0_), channel_id=1, source_target_pairs={{0,24},{4,28},{8,0},{12,4},{16,8},{20,12},{24,16},{28,20},{1,25},{... | collective-permute-start | bytes 1179656 | tf_op jit(solution)/shard_map/ppermute | solution.py:302
  115.9 1.4 copy-done.1
  117.3 1.1 copy-done.4
  118.4 5.1 %shard_map.86.refs_0_ = bf16[384,512]{1,0:T(8,128)(2,1)S(1)} custom-call(s32[5]{0:T(128)S(1)} %pad_add_fusion.2.info_ref, bf16[1024,768]{1,0:T(8,128)(2,1)S(1)} %copy-done.1, bf16[1024,768]{1,0:T(8,128)(2,1)S(1)} %copy-done.1, bf16[1024,768]{1,0:T(8,128)(2,1)S(1)} %copy-done.1, bf16[384,1024]{1,0:T(8,128)(2,1)S(1)} %copy-done.4), custom_call_target="tpu_custom_call" | custom-call | flops 805306368 | bytes 4000000 | tf_op jit(solution)/shard_map/pallas_call | solution.py:187
  123.8 2.7 %collective-permute-start.13 = (bf16[576,512]{1,0:T(8,128)(2,1)S(1)}, bf16[576,512]{1,0:T(8,128)(2,1)S(1)}, u32[]{:S(2)}, u32[]{:S(2)}) collective-permute-start(bf16[576,512]{1,0:T(8,128)(2,1)S(1)} %get-tuple-element.73), channel_id=1, source_target_pairs={{0,24},{4,28},{8,0},{12,4},{16,8},{20,12},{24,16},{28,20},{1,25},{... | collective-permute-start | bytes 1769480 | tf_op jit(solution)/shard_map/ppermute | solution.py:302
  126.4 10.4 %collective-permute-done.11.refs_1_.refs_3_ = bf16[576,512]{1,0:T(8,128)(2,1)S(1)} collective-permute-done((bf16[576,512]{1,0:T(8,128)(2,1)S(1)}, bf16[576,512]{1,0:T(8,128)(2,1)S(1)}, u32[]{:S(2)}, u32[]{:S(2)}) %collective-permute-start.11) | collective-permute-done | bytes 589856 | tf_op jit(solution)/shard_map/ppermute | solution.py:302
  136.8 0.7 slice.68
  137.5 0.7 slice.69
  138.2 2.7 %collective-permute-start.15 = (bf16[192,512]{1,0:T(8,128)(2,1)}, bf16[192,512]{1,0:T(8,128)(2,1)}, u32[]{:S(2)}, u32[]{:S(2)}) collective-permute-start(bf16[192,512]{1,0:T(8,128)(2,1)} %slice.69), channel_id=1, source_target_pairs={{0,24},{4,28},{8,0},{12,4},{16,8},{20,12},{24,16},{28,20},{1,25},{... | collective-permute-start | bytes 589832 | tf_op jit(solution)/shard_map/ppermute | solution.py:302
  140.9 1.0 copy-done.5
  141.9 5.0 %shard_map.89 = (f32[400,512]{1,0:T(8,128)S(1)}, bf16[400,512]{1,0:T(8,128)(2,1)S(1)}) custom-call(s32[8]{0:T(128)S(1)} %stack.64.info_ref, bf16[384,512]{1,0:T(8,128)(2,1)S(1)} %copy-done.5, bf16[384,512]{1,0:T(8,128)(2,1)S(1)} %collective-permute-done.10.refs_1_, bf16[384,512]{1,0:T(8,128)(2,1)S(1)} %collective-permute-done.12.refs_2_, ...), custom_call_target="tpu_custom_call" | custom-call | flops 1258291200 | bytes 6000000 | tf_op jit(solution)/shard_map/pallas_call | solution.py:237
  146.9 4.5 %collective-permute-start.18 = (bf16[400,512]{1,0:T(8,128)(2,1)S(1)}, bf16[400,512]{1,0:T(8,128)(2,1)S(1)}, u32[]{:S(2)}, u32[]{:S(2)}) collective-permute-start(bf16[400,512]{1,0:T(8,128)(2,1)S(1)} %get-tuple-element.62), channel_id=1, source_target_pairs={{0,4},{4,0},{8,12},{12,8},{16,20},{20,16},{24,28},{28,24},{1,5},{5... | collective-permute-start | bytes 1228808 | tf_op jit(solution)/shard_map/ppermute | solution.py:373
  151.5 4.7 %shard_map.87 = (f32[400,512]{1,0:T(8,128)S(1)}, bf16[400,512]{1,0:T(8,128)(2,1)S(1)}) custom-call(s32[8]{0:T(128)S(1)} %stack.64.info_ref, bf16[384,512]{1,0:T(8,128)(2,1)S(1)} %shard_map.86.refs_0_, bf16[576,512]{1,0:T(8,128)(2,1)S(1)} %collective-permute-done.11.refs_1_.refs_3_, bf16[576,512]{1,0:T(8,128)(2,1)S(1)} %collective-permute-done.13.refs_2_.refs_4_, ...), custom_call_target="tpu_custom_call" | custom-call | flops 1258291200 | bytes 6000000 | tf_op jit(solution)/shard_map/pallas_call | solution.py:237
  156.4 0.8 shard_map.90
  157.1 2.3 %collective-permute-start.19 = (bf16[400,128]{1,0:T(8,128)(2,1)S(1)}, bf16[400,128]{1,0:T(8,128)(2,1)S(1)}, u32[]{:S(2)}, u32[]{:S(2)}) collective-permute-start(bf16[400,128]{1,0:T(8,128)(2,1)S(1)} %get-tuple-element.63), channel_id=1, source_target_pairs={{0,64},{32,96},{64,128},{96,160},{128,192},{160,224},{192,0},{224,... | collective-permute-start | bytes 307208 | tf_op jit(solution)/shard_map/ppermute | solution.py:302
  159.4 5.6 %collective-permute-start.20 = (bf16[400,128]{1,0:T(8,128)(2,1)S(1)}, bf16[400,128]{1,0:T(8,128)(2,1)S(1)}, u32[]{:S(2)}, u32[]{:S(2)}) collective-permute-start(bf16[400,128]{1,0:T(8,128)(2,1)S(1)} %get-tuple-element.64), channel_id=1, source_target_pairs={{0,96},{32,128},{64,160},{96,192},{128,224},{160,0},{192,32},{224,... | collective-permute-start | bytes 307208 | tf_op jit(solution)/shard_map/ppermute | solution.py:302
  165.0 2.1 %collective-permute-start.21 = (bf16[400,128]{1,0:T(8,128)(2,1)S(1)}, bf16[400,128]{1,0:T(8,128)(2,1)S(1)}, u32[]{:S(2)}, u32[]{:S(2)}) collective-permute-start(bf16[400,128]{1,0:T(8,128)(2,1)S(1)} %get-tuple-element.65), channel_id=1, source_target_pairs={{0,128},{32,160},{64,192},{96,224},{128,0},{160,32},{192,64},{224,... | collective-permute-start | bytes 307208 | tf_op jit(solution)/shard_map/ppermute | solution.py:302
  167.1 2.2 %collective-permute-start.22 = (bf16[400,128]{1,0:T(8,128)(2,1)S(1)}, bf16[400,128]{1,0:T(8,128)(2,1)S(1)}, u32[]{:S(2)}, u32[]{:S(2)}) collective-permute-start(bf16[400,128]{1,0:T(8,128)(2,1)S(1)} %get-tuple-element.66), channel_id=1, source_target_pairs={{0,160},{32,192},{64,224},{96,0},{128,32},{160,64},{192,96},{224,1... | collective-permute-start | bytes 307208 | tf_op jit(solution)/shard_map/ppermute | solution.py:302
  169.3 0.8 shard_map.88
  170.1 0.3 collective-permute-start.17
  170.4 2.9 %collective-permute-start.23 = (bf16[400,128]{1,0:T(8,128)(2,1)S(1)}, bf16[400,128]{1,0:T(8,128)(2,1)S(1)}, u32[]{:S(2)}, u32[]{:S(2)}) collective-permute-start(bf16[400,128]{1,0:T(8,128)(2,1)S(1)} %get-tuple-element.67), channel_id=1, source_target_pairs={{0,192},{32,224},{64,0},{96,32},{128,64},{160,96},{192,128},{224,1... | collective-permute-start | bytes 307208 | tf_op jit(solution)/shard_map/ppermute | solution.py:302
  173.3 3.2 %collective-permute-done.20.refs_3_ = bf16[400,128]{1,0:T(8,128)(2,1)S(1)} collective-permute-done((bf16[400,128]{1,0:T(8,128)(2,1)S(1)}, bf16[400,128]{1,0:T(8,128)(2,1)S(1)}, u32[]{:S(2)}, u32[]{:S(2)}) %collective-permute-start.20) | collective-permute-done | bytes 102432 | tf_op jit(solution)/shard_map/ppermute | solution.py:302
  176.5 2.2 %collective-permute-done.22.refs_5_ = bf16[400,128]{1,0:T(8,128)(2,1)S(1)} collective-permute-done((bf16[400,128]{1,0:T(8,128)(2,1)S(1)}, bf16[400,128]{1,0:T(8,128)(2,1)S(1)}, u32[]{:S(2)}, u32[]{:S(2)}) %collective-permute-start.22) | collective-permute-done | bytes 102432 | tf_op jit(solution)/shard_map/ppermute | solution.py:302
  178.7 3.0 %collective-permute-done.17.refs_1_ = bf16[400,128]{1,0:T(8,128)(2,1)S(1)} collective-permute-done((bf16[400,128]{1,0:T(8,128)(2,1)S(1)}, bf16[400,128]{1,0:T(8,128)(2,1)S(1)}, u32[]{:S(2)}, u32[]{:S(2)}) %collective-permute-start.17) | collective-permute-done | bytes 102432 | tf_op jit(solution)/shard_map/ppermute | solution.py:302
  181.7 3.1 %collective-permute-done.23.refs_6_ = bf16[400,128]{1,0:T(8,128)(2,1)S(1)} collective-permute-done((bf16[400,128]{1,0:T(8,128)(2,1)S(1)}, bf16[400,128]{1,0:T(8,128)(2,1)S(1)}, u32[]{:S(2)}, u32[]{:S(2)}) %collective-permute-start.23) | collective-permute-done | bytes 102432 | tf_op jit(solution)/shard_map/ppermute | solution.py:302
  184.7 0.2 collective-permute-done.24.refs_7_
  185.0 1.6 shard_map.91
  (72 shorter events, 1.2 us)
Async XLA Ops:
  6.5 41.8 %all-gather.11.cloned.1.call-start = ((), (), s32[]{:S(2)}) async-start(), calls=%async_computation.2 | async-start | bytes 1437696 | tf_op jit(solution)/shard_map/all_gather | solution.py:320
  8.2 83.1 %all-gather.7.cloned.1.call-start = ((), (), s32[]{:S(2)}) async-start(), calls=%async_computation | async-start | bytes 2764800 | tf_op jit(solution)/shard_map/all_gather | solution.py:336
  8.3 1.5 collective-permute-start
  9.9 6.1 %collective-permute-start.1 = (bf16[100,768]{1,0:T(8,128)(2,1)S(1)}, bf16[100,768]{1,0:T(8,128)(2,1)S(1)}, u32[]{:S(2)}, u32[]{:S(2)}) collective-permute-start(bf16[100,768]{1,0:T(8,128)(2,1)S(1)} %pad_maximum_fusion.2), channel_id=1, source_target_pairs={{0,1},{1,2},{2,3},{3,0},{4,5},{5,6},{6,7},{7,4},{8,9},{9,10},{10,1... | collective-permute-start | bytes 460808 | tf_op jit(solution)/shard_map/ppermute | solution.py:302
  12.0 4.1 %collective-permute-start.2 = (bf16[100,768]{1,0:T(8,128)(2,1)S(1)}, bf16[100,768]{1,0:T(8,128)(2,1)S(1)}, u32[]{:S(2)}, u32[]{:S(2)}) collective-permute-start(bf16[100,768]{1,0:T(8,128)(2,1)S(1)} %pad_maximum_fusion.2), channel_id=1, source_target_pairs={{0,3},{1,0},{2,1},{3,2},{4,7},{5,4},{6,5},{7,6},{8,11},{9,8},{10,9... | collective-permute-start | bytes 460808 | tf_op jit(solution)/shard_map/ppermute | solution.py:302
  13.4 7.2 %collective-permute-start.3 = (bf16[100,768]{1,0:T(8,128)(2,1)S(1)}, bf16[100,768]{1,0:T(8,128)(2,1)S(1)}, u32[]{:S(2)}, u32[]{:S(2)}) collective-permute-start(bf16[100,768]{1,0:T(8,128)(2,1)S(1)} %pad_maximum_fusion.2), channel_id=1, source_target_pairs={{0,2},{1,3},{2,0},{3,1},{4,6},{5,7},{6,4},{7,5},{8,10},{9,11},{10,... | collective-permute-start | bytes 460808 | tf_op jit(solution)/shard_map/ppermute | solution.py:302
  21.7 3.3 %copy-start.15 = (f32[3200]{0:T(1024)S(1)}, f32[3200]{0:T(1024)}, u32[]{:S(2)}) copy-start(f32[3200]{0:T(1024)} %param.10) | copy-start | bytes 38404
  21.7 3.3 %copy-start.17 = (s32[8]{0:T(128)S(1)}, s32[8]{0:T(128)}, u32[]{:S(2)}) copy-start(s32[8]{0:T(128)} %constant.105.clone) | copy-start | bytes 100
  21.7 119.2 %all-gather.9.cloned.1.call-start = ((), (), s32[]{:S(2)}) async-start(), calls=%async_computation.1 | async-start | bytes 2764800 | tf_op jit(solution)/shard_map/all_gather | solution.py:354
  26.5 2.9 %copy-start.2 = (bf16[1,1024,3200]{2,1,0:T(8,128)(2,1)S(1)}, bf16[1,1024,3200]{2,1,0:T(8,128)(2,1)}, u32[]{:S(2)}) copy-start(bf16[1,1024,3200]{2,1,0:T(8,128)(2,1)} %param.8) | copy-start | bytes 19660804
  36.6 2.9 %copy-start = (bf16[4,1024,800]{2,1,0:T(8,128)(2,1)}, bf16[4,1024,800]{2,1,0:T(8,128)(2,1)S(1)}, u32[]{:S(2)}) copy-start(bf16[4,1024,800]{2,1,0:T(8,128)(2,1)S(1)} %get-tuple-element.46.refs_0_.refs_1_.refs_2_.x_ref) | copy-start | bytes 19660804
  39.5 2.8 %copy-start.3 = (bf16[1024,3200]{1,0:T(8,128)(2,1)}, bf16[1024,3200]{1,0:T(8,128)(2,1)S(1)}, u32[]{:S(2)}) copy-start(bf16[1024,3200]{1,0:T(8,128)(2,1)S(1)} %get-tuple-element.49.normed) | copy-start | bytes 19660804
  43.0 7.0 %copy-start.16 = (f32[400]{0:T(512)S(1)}, f32[400]{0:T(512)}, u32[]{:S(2)}) copy-start(f32[400]{0:T(512)} %param.13) | copy-start | bytes 4804
  49.8 15.2 %copy-start.7 = (bf16[400,768]{1,0:T(8,128)(2,1)}, bf16[400,768]{1,0:T(8,128)(2,1)S(1)}, u32[]{:S(2)}) copy-start(bf16[400,768]{1,0:T(8,128)(2,1)S(1)} %reshape.36.refs_1_) | copy-start | bytes 1843204
  50.0 15.0 %copy-start.8 = (bf16[400,768]{1,0:T(8,128)(2,1)}, bf16[400,768]{1,0:T(8,128)(2,1)S(1)}, u32[]{:S(2)}) copy-start(bf16[400,768]{1,0:T(8,128)(2,1)S(1)} %reshape.37.refs_2_) | copy-start | bytes 1843204
  50.1 12.2 %collective-permute-start.4 = (bf16[400,768]{1,0:T(8,128)(2,1)S(1)}, bf16[400,768]{1,0:T(8,128)(2,1)S(1)}, u32[]{:S(2)}, u32[]{:S(2)}) collective-permute-start(bf16[400,768]{1,0:T(8,128)(2,1)S(1)} %reshape.36.refs_1_), channel_id=1, source_target_pairs={{0,1},{1,2},{2,3},{3,0},{4,5},{5,6},{6,7},{7,4},{8,9},{9,10},{10,1... | collective-permute-start | bytes 1843208 | tf_op jit(solution)/shard_map/ppermute | solution.py:302
  51.4 10.9 %collective-permute-start.7 = (bf16[400,768]{1,0:T(8,128)(2,1)S(1)}, bf16[400,768]{1,0:T(8,128)(2,1)S(1)}, u32[]{:S(2)}, u32[]{:S(2)}) collective-permute-start(bf16[400,768]{1,0:T(8,128)(2,1)S(1)} %reshape.37.refs_2_), channel_id=1, source_target_pairs={{0,3},{1,0},{2,1},{3,2},{4,7},{5,4},{6,5},{7,6},{8,11},{9,8},{10,9... | collective-permute-start | bytes 1843208 | tf_op jit(solution)/shard_map/ppermute | solution.py:302
  52.9 22.6 %collective-permute-start.5 = (bf16[400,768]{1,0:T(8,128)(2,1)S(1)}, bf16[400,768]{1,0:T(8,128)(2,1)S(1)}, u32[]{:S(2)}, u32[]{:S(2)}) collective-permute-start(bf16[400,768]{1,0:T(8,128)(2,1)S(1)} %reshape.37.refs_2_), channel_id=1, source_target_pairs={{0,1},{1,2},{2,3},{3,0},{4,5},{5,6},{6,7},{7,4},{8,9},{9,10},{10,1... | collective-permute-start | bytes 1843208 | tf_op jit(solution)/shard_map/ppermute | solution.py:302
  52.9 22.6 %collective-permute-start.6 = (bf16[400,768]{1,0:T(8,128)(2,1)S(1)}, bf16[400,768]{1,0:T(8,128)(2,1)S(1)}, u32[]{:S(2)}, u32[]{:S(2)}) collective-permute-start(bf16[400,768]{1,0:T(8,128)(2,1)S(1)} %reshape.36.refs_1_), channel_id=1, source_target_pairs={{0,3},{1,0},{2,1},{3,2},{4,7},{5,4},{6,5},{7,6},{8,11},{9,8},{10,9... | collective-permute-start | bytes 1843208 | tf_op jit(solution)/shard_map/ppermute | solution.py:302
  62.3 8.2 %copy-start.10 = (bf16[400,768]{1,0:T(8,128)(2,1)}, bf16[400,768]{1,0:T(8,128)(2,1)S(1)}, u32[]{:S(2)}) copy-start(bf16[400,768]{1,0:T(8,128)(2,1)S(1)} %collective-permute-done.4.refs_3_) | copy-start | bytes 1843204
  62.3 26.4 %collective-permute-start.8 = (bf16[400,768]{1,0:T(8,128)(2,1)S(1)}, bf16[400,768]{1,0:T(8,128)(2,1)S(1)}, u32[]{:S(2)}, u32[]{:S(2)}) collective-permute-start(bf16[400,768]{1,0:T(8,128)(2,1)S(1)} %collective-permute-done.4.refs_3_), channel_id=1, source_target_pairs={{0,1},{1,2},{2,3},{3,0},{4,5},{5,6},{6,7},{7,4},{8,9},{9,10},{10,1... | collective-permute-start | bytes 1843208 | tf_op jit(solution)/shard_map/ppermute | solution.py:302
  62.3 8.2 %copy-start.11 = (bf16[400,768]{1,0:T(8,128)(2,1)}, bf16[400,768]{1,0:T(8,128)(2,1)S(1)}, u32[]{:S(2)}) copy-start(bf16[400,768]{1,0:T(8,128)(2,1)S(1)} %collective-permute-done.7.refs_6_) | copy-start | bytes 1843204
  62.3 26.4 %collective-permute-start.9 = (bf16[400,768]{1,0:T(8,128)(2,1)S(1)}, bf16[400,768]{1,0:T(8,128)(2,1)S(1)}, u32[]{:S(2)}, u32[]{:S(2)}) collective-permute-start(bf16[400,768]{1,0:T(8,128)(2,1)S(1)} %collective-permute-done.7.refs_6_), channel_id=1, source_target_pairs={{0,3},{1,0},{2,1},{3,2},{4,7},{5,4},{6,5},{7,6},{8,11},{9,8},{10,9... | collective-permute-start | bytes 1843208 | tf_op jit(solution)/shard_map/ppermute | solution.py:302
  75.5 0.8 copy-start.13
  76.3 0.8 copy-start.14
  88.7 2.6 %copy-start.9 = (bf16[400,768]{1,0:T(8,128)(2,1)}, bf16[400,768]{1,0:T(8,128)(2,1)S(1)}, u32[]{:S(2)}) copy-start(bf16[400,768]{1,0:T(8,128)(2,1)S(1)} %collective-permute-done.8.top) | copy-start | bytes 1843204
  88.7 2.6 %copy-start.12 = (bf16[400,768]{1,0:T(8,128)(2,1)}, bf16[400,768]{1,0:T(8,128)(2,1)S(1)}, u32[]{:S(2)}) copy-start(bf16[400,768]{1,0:T(8,128)(2,1)S(1)} %collective-permute-done.9.low) | copy-start | bytes 1843204
  107.5 16.1 %collective-permute-start.10 = (bf16[384,512]{1,0:T(8,128)(2,1)}, bf16[384,512]{1,0:T(8,128)(2,1)S(1)}, u32[]{:S(2)}, u32[]{:S(2)}) collective-permute-start(bf16[384,512]{1,0:T(8,128)(2,1)} %get-tuple-element.52.refs_0_), channel_id=1, source_target_pairs={{0,8},{4,12},{8,16},{12,20},{16,24},{20,28},{24,0},{28,4},{1,9},{5... | collective-permute-start | bytes 1179656 | tf_op jit(solution)/shard_map/ppermute | solution.py:302
  108.7 14.9 %collective-permute-start.12 = (bf16[384,512]{1,0:T(8,128)(2,1)}, bf16[384,512]{1,0:T(8,128)(2,1)S(1)}, u32[]{:S(2)}, u32[]{:S(2)}) collective-permute-start(bf16[384,512]{1,0:T(8,128)(2,1)} %get-tuple-element.52.refs_0_), channel_id=1, source_target_pairs={{0,24},{4,28},{8,0},{12,4},{16,8},{20,12},{24,16},{28,20},{1,25},{... | collective-permute-start | bytes 1179656 | tf_op jit(solution)/shard_map/ppermute | solution.py:302
  115.9 1.4 copy-start.1
  117.3 1.1 copy-start.4
  123.7 13.1 %collective-permute-start.11 = (bf16[576,512]{1,0:T(8,128)(2,1)S(1)}, bf16[576,512]{1,0:T(8,128)(2,1)S(1)}, u32[]{:S(2)}, u32[]{:S(2)}) collective-permute-start(bf16[576,512]{1,0:T(8,128)(2,1)S(1)} %get-tuple-element.74), channel_id=1, source_target_pairs={{0,8},{4,12},{8,16},{12,20},{16,24},{20,28},{24,0},{28,4},{1,9},{5... | collective-permute-start | bytes 1769480 | tf_op jit(solution)/shard_map/ppermute | solution.py:302
  123.8 13.7 %collective-permute-start.13 = (bf16[576,512]{1,0:T(8,128)(2,1)S(1)}, bf16[576,512]{1,0:T(8,128)(2,1)S(1)}, u32[]{:S(2)}, u32[]{:S(2)}) collective-permute-start(bf16[576,512]{1,0:T(8,128)(2,1)S(1)} %get-tuple-element.73), channel_id=1, source_target_pairs={{0,24},{4,28},{8,0},{12,4},{16,8},{20,12},{24,16},{28,20},{1,25},{... | collective-permute-start | bytes 1769480 | tf_op jit(solution)/shard_map/ppermute | solution.py:302
  137.5 14.0 %collective-permute-start.14 = (bf16[192,512]{1,0:T(8,128)(2,1)}, bf16[192,512]{1,0:T(8,128)(2,1)}, u32[]{:S(2)}, u32[]{:S(2)}) collective-permute-start(bf16[192,512]{1,0:T(8,128)(2,1)} %slice.68), channel_id=1, source_target_pairs={{0,8},{4,12},{8,16},{12,20},{16,24},{20,28},{24,0},{28,4},{1,9},{5... | collective-permute-start | bytes 589832 | tf_op jit(solution)/shard_map/ppermute | solution.py:302
  138.2 13.3 %collective-permute-start.15 = (bf16[192,512]{1,0:T(8,128)(2,1)}, bf16[192,512]{1,0:T(8,128)(2,1)}, u32[]{:S(2)}, u32[]{:S(2)}) collective-permute-start(bf16[192,512]{1,0:T(8,128)(2,1)} %slice.69), channel_id=1, source_target_pairs={{0,24},{4,28},{8,0},{12,4},{16,8},{20,12},{24,16},{28,20},{1,25},{... | collective-permute-start | bytes 589832 | tf_op jit(solution)/shard_map/ppermute | solution.py:302
  140.9 1.0 copy-start.5
  146.9 9.4 %collective-permute-start.18 = (bf16[400,512]{1,0:T(8,128)(2,1)S(1)}, bf16[400,512]{1,0:T(8,128)(2,1)S(1)}, u32[]{:S(2)}, u32[]{:S(2)}) collective-permute-start(bf16[400,512]{1,0:T(8,128)(2,1)S(1)} %get-tuple-element.62), channel_id=1, source_target_pairs={{0,4},{4,0},{8,12},{12,8},{16,20},{20,16},{24,28},{28,24},{1,5},{5... | collective-permute-start | bytes 1228808 | tf_op jit(solution)/shard_map/ppermute | solution.py:373
  156.2 28.7 %copy-start.6 = (s32[4,8]{1,0:T(4,128)S(1)}, s32[4,8]{1,0:T(4,128)}, u32[]{:S(2)}) copy-start(s32[4,8]{1,0:T(4,128)} %order_ref.1) | copy-start | bytes 388
  156.2 13.1 %collective-permute-start.16 = (bf16[400,512]{1,0:T(8,128)(2,1)S(1)}, bf16[400,512]{1,0:T(8,128)(2,1)S(1)}, u32[]{:S(2)}, u32[]{:S(2)}) collective-permute-start(bf16[400,512]{1,0:T(8,128)(2,1)S(1)} %get-tuple-element.55), channel_id=1, source_target_pairs={{0,4},{4,0},{8,12},{12,8},{16,20},{20,16},{24,28},{28,24},{1,5},{5... | collective-permute-start | bytes 1228808 | tf_op jit(solution)/shard_map/ppermute | solution.py:373
  157.1 13.3 %collective-permute-start.19 = (bf16[400,128]{1,0:T(8,128)(2,1)S(1)}, bf16[400,128]{1,0:T(8,128)(2,1)S(1)}, u32[]{:S(2)}, u32[]{:S(2)}) collective-permute-start(bf16[400,128]{1,0:T(8,128)(2,1)S(1)} %get-tuple-element.63), channel_id=1, source_target_pairs={{0,64},{32,96},{64,128},{96,160},{128,192},{160,224},{192,0},{224,... | collective-permute-start | bytes 307208 | tf_op jit(solution)/shard_map/ppermute | solution.py:302
  159.4 17.1 %collective-permute-start.20 = (bf16[400,128]{1,0:T(8,128)(2,1)S(1)}, bf16[400,128]{1,0:T(8,128)(2,1)S(1)}, u32[]{:S(2)}, u32[]{:S(2)}) collective-permute-start(bf16[400,128]{1,0:T(8,128)(2,1)S(1)} %get-tuple-element.64), channel_id=1, source_target_pairs={{0,96},{32,128},{64,160},{96,192},{128,224},{160,0},{192,32},{224,... | collective-permute-start | bytes 307208 | tf_op jit(solution)/shard_map/ppermute | solution.py:302
  165.0 11.5 %collective-permute-start.21 = (bf16[400,128]{1,0:T(8,128)(2,1)S(1)}, bf16[400,128]{1,0:T(8,128)(2,1)S(1)}, u32[]{:S(2)}, u32[]{:S(2)}) collective-permute-start(bf16[400,128]{1,0:T(8,128)(2,1)S(1)} %get-tuple-element.65), channel_id=1, source_target_pairs={{0,128},{32,160},{64,192},{96,224},{128,0},{160,32},{192,64},{224,... | collective-permute-start | bytes 307208 | tf_op jit(solution)/shard_map/ppermute | solution.py:302
  167.1 11.6 %collective-permute-start.22 = (bf16[400,128]{1,0:T(8,128)(2,1)S(1)}, bf16[400,128]{1,0:T(8,128)(2,1)S(1)}, u32[]{:S(2)}, u32[]{:S(2)}) collective-permute-start(bf16[400,128]{1,0:T(8,128)(2,1)S(1)} %get-tuple-element.66), channel_id=1, source_target_pairs={{0,160},{32,192},{64,224},{96,0},{128,32},{160,64},{192,96},{224,1... | collective-permute-start | bytes 307208 | tf_op jit(solution)/shard_map/ppermute | solution.py:302
  170.1 11.6 %collective-permute-start.17 = (bf16[400,128]{1,0:T(8,128)(2,1)S(1)}, bf16[400,128]{1,0:T(8,128)(2,1)S(1)}, u32[]{:S(2)}, u32[]{:S(2)}) collective-permute-start(bf16[400,128]{1,0:T(8,128)(2,1)S(1)} %get-tuple-element.59), channel_id=1, source_target_pairs={{0,32},{32,64},{64,96},{96,128},{128,160},{160,192},{192,224},{224... | collective-permute-start | bytes 307208 | tf_op jit(solution)/shard_map/ppermute | solution.py:302
  170.4 14.3 %collective-permute-start.23 = (bf16[400,128]{1,0:T(8,128)(2,1)S(1)}, bf16[400,128]{1,0:T(8,128)(2,1)S(1)}, u32[]{:S(2)}, u32[]{:S(2)}) collective-permute-start(bf16[400,128]{1,0:T(8,128)(2,1)S(1)} %get-tuple-element.67), channel_id=1, source_target_pairs={{0,192},{32,224},{64,0},{96,32},{128,64},{160,96},{192,128},{224,1... | collective-permute-start | bytes 307208 | tf_op jit(solution)/shard_map/ppermute | solution.py:302
  176.5 8.4 %collective-permute-start.24 = (bf16[400,128]{1,0:T(8,128)(2,1)S(1)}, bf16[400,128]{1,0:T(8,128)(2,1)S(1)}, u32[]{:S(2)}, u32[]{:S(2)}) collective-permute-start(bf16[400,128]{1,0:T(8,128)(2,1)S(1)} %get-tuple-element.68), channel_id=1, source_target_pairs={{0,224},{32,0},{64,32},{96,64},{128,96},{160,128},{192,160},{224,1... | collective-permute-start | bytes 307208 | tf_op jit(solution)/shard_map/ppermute | solution.py:302
Sparse Core Ops, SparseCore 0:
  9.1 39.1 all-gather.10
  50.1 41.1 all-gather.6
  93.1 40.7 all-gather.8

commit v2 on v1

--- a/solution.py
+++ b/solution.py
@@ -11,7 +11,7 @@
 HD = 128
 BF = jnp.bfloat16
 F32 = jnp.float32
-ORDER = (4, 3, 5, 2, 6, 1, 7, 0)
+ORDER = (5, 3, 4, 2, 6, 7, 1, 0)
 
 
 def norm_body(x_ref, gain_ref, plain, by_dp):
@@ -21,7 +21,8 @@
     plain[...] = y
     for s in range(8):
         for d in range(4):
-            by_dp[d, :, s * 100 : s * 100 + 100] = y[:, (s * 4 + d) * 100 : (s * 4 + d) * 100 + 100]
+            at = s % 4 * 100
+            by_dp[d * 2 + s // 4, :, at : at + 100] = y[:, (s * 4 + d) * 100 : (s * 4 + d) * 100 + 100]
 
 
 def normalise(x, gain):
@@ -36,11 +37,11 @@
         ],
         out_specs=[
             pl.BlockSpec((tile, wide), lambda r: (r, 0)),
-            pl.BlockSpec((4, tile, 800), lambda r: (0, r, 0)),
+            pl.BlockSpec((8, tile, 400), lambda r: (0, r, 0)),
         ],
         out_shape=[
             jax.ShapeDtypeStruct((rows, wide), BF),
-            jax.ShapeDtypeStruct((4, rows, 800), BF),
+            jax.ShapeDtypeStruct((8, rows, 400), BF),
         ],
         compiler_params=pltpu.CompilerParams(vmem_limit_bytes=16 * 2**20),
         cost_estimate=pl.CostEstimate(flops=30_000_000, bytes_accessed=20_000_000, transcendentals=1024),
@@ -53,9 +54,9 @@
     blocks = refs[len(sums) : len(sums) + pairs]
     total = sums[0][...] if sums else None
     for k in range(pairs):
-        term = jnp.dot(blocks[k][0, :, :400], halves[2 * k][...], preferred_element_type=F32)
+        term = jnp.dot(blocks[k][0], halves[2 * k][...], preferred_element_type=F32)
         total = term if total is None else total + term
-        total += jnp.dot(blocks[k][0, :, 400:], halves[2 * k + 1][...], preferred_element_type=F32)
+        total += jnp.dot(blocks[k][1], halves[2 * k + 1][...], preferred_element_type=F32)
     out_ref[...] = total
 
 
@@ -66,7 +67,7 @@
     tile = rows // 4
     part = pl.BlockSpec((tile, wide), lambda r, a: (r, 0))
     blocks = [
-        pl.BlockSpec((1, tile, deep), lambda r, a, k=k: (a[k], r, 0)) for k in range(pairs)
+        pl.BlockSpec((2, tile, deep), lambda r, a, k=k: (a[k], r, 0)) for k in range(pairs)
     ]
     return pl.pallas_call(
         early_body,
@@ -75,13 +76,13 @@
             grid=(rows // tile,),
             in_specs=[part] * len(sums)
             + blocks
-            + [pl.BlockSpec((deep // 2, wide), lambda r, a: (0, 0))] * len(halves),
+            + [pl.BlockSpec((deep, wide), lambda r, a: (0, 0))] * len(halves),
             out_specs=part,
         ),
         out_shape=jax.ShapeDtypeStruct((rows, wide), F32),
-        compiler_params=pltpu.CompilerParams(vmem_limit_bytes=54 * 2**20),
+        compiler_params=pltpu.CompilerParams(vmem_limit_bytes=40 * 2**20),
         cost_estimate=pl.CostEstimate(
-            flops=2 * pairs * rows * deep * wide, bytes_accessed=10_000_000, transcendentals=0
+            flops=4 * pairs * rows * deep * wide, bytes_accessed=10_000_000, transcendentals=0
         ),
     )(at, *sums, *[by_dp] * pairs, *halves)
 
@@ -111,11 +112,11 @@
 
     @pl.when(step < 4)
     def _():
-        total = sums[...] + jnp.dot(x_ref[0, :, :400], top[...], preferred_element_type=F32)
-        total += jnp.dot(x_ref[0, :, 400:], low[...], preferred_element_type=F32)
+        total = sums[...] + jnp.dot(x_ref[0], top[...], preferred_element_type=F32)
+        total += jnp.dot(x_ref[1], low[...], preferred_element_type=F32)
         qk_ref[...] = total.astype(BF)
         value = jnp.dot(normed[...], w_ref[...], preferred_element_type=F32)
-        vt_ref[...] = value.T.astype(BF)
+        vt_ref[...] = value.astype(BF).T
 
     for r in range(4):
 
@@ -138,7 +139,7 @@
     deep, tall = by_dp.shape[2], normed.shape[1]
     narrow = w_v.shape[1]
     tile = rows // 4
-    half = pl.BlockSpec((deep // 2, wide), lambda r, a: (0, 0))
+    half = pl.BlockSpec((deep, wide), lambda r, a: (0, 0))
 
     def upto(r):
         return jnp.minimum(r, 3)
@@ -150,7 +151,7 @@
             grid=(6,),
             in_specs=[
                 pl.BlockSpec((tile, wide), lambda r, a: (upto(r), 0)),
-                pl.BlockSpec((1, tile, deep), lambda r, a: (a[3], upto(r), 0)),
+                pl.BlockSpec((2, tile, deep), lambda r, a: (a[3], upto(r), 0)),
                 half,
                 half,
                 pl.BlockSpec((tile, tall), lambda r, a: (upto(r), 0)),
@@ -168,7 +169,7 @@
             jax.ShapeDtypeStruct((narrow, rows), BF),
             jax.ShapeDtypeStruct((narrow, 512), BF),
         ],
-        compiler_params=pltpu.CompilerParams(vmem_limit_bytes=58 * 2**20),
+        compiler_params=pltpu.CompilerParams(vmem_limit_bytes=48 * 2**20),
         cost_estimate=pl.CostEstimate(
             flops=2 * rows * (deep * wide + tall * narrow) + 2 * rows * rows * narrow,
             bytes_accessed=18_000_000,
@@ -278,12 +279,12 @@
 
 def deliver_body(info_ref, order_ref, *refs):
     out_ref = refs[8]
-    for k in range(8):
+    for i, k in enumerate(ORDER[::-1]):
         source = (info_ref[0] - k + 8) % 8
         slot = 0
         for j in range(8):
             slot = jnp.where(order_ref[info_ref[1], j] == source, j, slot)
-        out_ref[slot] = refs[k][...]
+        out_ref[slot] = refs[i][...]
 
 
 def deliver(info, order, pieces):
@@ -387,7 +388,7 @@
     sent(0, encoded(0, ((ctx0, 0, 0, 0, 384), (back, 0, 1, 0, 384), (ahead, 0, 2, 0, 384)) + far))
     far = ((top, 0, 3, 0, 192), (low, 0, 3, 192, 192))
     sent(1, encoded(1, ((ctx1, 0, 0, 0, 384), (up, 0, 1, 0, 384), (down, 0, 2, 0, 384)) + far))
-    arranged = deliver(place_info, order, [received[k] for k in range(8)])
+    arranged = deliver(place_info, order, [received[k] for k in ORDER[::-1]])
     return arranged.transpose(0, 2, 1)[None]
 
 

time: 195 us -> 191 us (0.979)
  Pallas kernels: 55.6 us -> 48.3 us
  starting transfers between devices: 48.7 us -> 54.3 us
    pallas_call x2, Pallas kernels: 14.3 us -> 8.47 us  [early(): pl.pallas_call(early_body, grid_spec=pltpu.PrefetchScalarGridSpec(num_sca...]
    ppermute x22, starting transfers between devices: 42.4 us -> 47.8 us  [around(): return lax.ppermute(x, axis, [(i, (i + step) % size) for i in range(size)])]
    ppermute x22, waiting for transfers between devices: 42.1 us -> 39.6 us  [around(): return lax.ppermute(x, axis, [(i, (i + step) % size) for i in range(size)])]
    unnamed x36 -> x26, local copies, waits for them, and re-layouts: 13.8 us -> 16 us
  transfers between devices with their start and end apart: 28 -> 28, of which waited for: 14 -> 13; matrix products, arithmetic and copies ran while one was open for 5% -> 4% of each run, Pallas kernels for 28% -> 25%
where the time goes in v2:
time: 191 us
  starting transfers between devices  54.3 us (28%)
  waiting for transfers between devices  48.3 us (25%)
  Pallas kernels  48.3 us (25%)
  local copies, waits for them, and re-layouts  24.5 us (13%)
  between operations  14.2 us (7%)
    ppermute x22, starting transfers between devices, around(): return lax.ppermute(x, axis, [(i, (i + step) % size) for i in range(size)])  47.8 us
    ppermute x22, waiting for transfers between devices, around(): return lax.ppermute(x, axis, [(i, (i + step) % size) for i in range(size)])  39.6 us
    unnamed x26, local copies, waits for them, and re-layouts  16 us
    pallas_call x1, Pallas kernels, late(): pl.pallas_call(late_body, grid_spec=pltpu.PrefetchScalarGridSpec(num_scal...  14.4 us
    pallas_call x2, Pallas kernels, project(): pl.pallas_call(functools.partial(project_body, [part[1:] for part in part...  10.1 us
    pallas_call x2, Pallas kernels, early(): pl.pallas_call(early_body, grid_spec=pltpu.PrefetchScalarGridSpec(num_sca...  8.47 us
    pallas_call x1, Pallas kernels, normalise(): pl.pallas_call(norm_body, grid=(rows // tile,), in_specs=[pl.BlockSpec((t...  7.18 us
    all_gather x1, waiting for transfers between devices, shards(): block_b = lax.all_gather(w_b, 'section', axis=0, tiled=False)  6.07 us
  transfers between devices with their start and end apart: 28, of which 13 were waited for; matrix products, arithmetic and copies ran while one was open for 4% of the time, Pallas kernels for 25%

profile of v2, /device:TPU:1, one launch (start us, length us, event | category | flops | bytes accessed | tf_op | source)
XLA Modules:
  0.0 190.7 jit_solution(10413737366441442810)
XLA Ops:
  6.5 1.0 slice_bitcast_fusion
  7.5 0.7 maximum_bitcast_fusion
  8.3 1.5 collective-permute-start
  9.8 2.1 %collective-permute-start.1 = (bf16[100,768]{1,0:T(8,128)(2,1)S(1)}, bf16[100,768]{1,0:T(8,128)(2,1)S(1)}, u32[]{:S(2)}, u32[]{:S(2)}) collective-permute-start(bf16[100,768]{1,0:T(8,128)(2,1)S(1)} %pad_maximum_fusion.2), channel_id=1, source_target_pairs={{0,1},{1,2},{2,3},{3,0},{4,5},{5,6},{6,7},{7,4},{8,9},{9,10},{10,1... | collective-permute-start | bytes 460808 | tf_op jit(solution)/shard_map/ppermute | solution.py:303
  12.0 1.4 collective-permute-start.2
  13.4 1.6 collective-permute-start.3
  15.0 0.9 collective-permute-done.1
  15.9 0.2 collective-permute-done.2
  16.1 4.5 %collective-permute-done.3 = bf16[100,768]{1,0:T(8,128)(2,1)S(1)} collective-permute-done((bf16[100,768]{1,0:T(8,128)(2,1)S(1)}, bf16[100,768]{1,0:T(8,128)(2,1)S(1)}, u32[]{:S(2)}, u32[]{:S(2)}) %collective-permute-start.3) | collective-permute-done | bytes 153632 | tf_op jit(solution)/shard_map/ppermute | solution.py:303
  20.6 0.1 reshape.17
  20.8 0.9 fusion.2
  22.5 1.8 constant_dynamic-slice_fusion
  24.3 0.6 copy.12
  25.0 0.7 gather_fusion
  25.9 2.9 %copy-done.3 = bf16[1,1024,3200]{2,1,0:T(8,128)(2,1)S(1)} copy-done((bf16[1,1024,3200]{2,1,0:T(8,128)(2,1)S(1)}, bf16[1,1024,3200]{2,1,0:T(8,128)(2,1)}, u32[]{:S(2)}) %copy-start.3) | copy-done | bytes 6553624
  28.8 7.2 %shard_map.82 = (bf16[1024,3200]{1,0:T(8,128)(2,1)S(1)}, bf16[8,1024,400]{2,1,0:T(8,128)(2,1)S(1)}) custom-call(bf16[1024,3200]{1,0:T(8,128)(2,1)S(1)} %bitcast.37, f32[1,3200]{1,0:T(1,128)S(1)} %broadcast_in_dim.36.gain_ref), custom_call_target="tpu_custom_call" | custom-call | flops 30000000 | bytes 20000000 | tf_op jit(solution)/shard_map/pallas_call | solution.py:31
  36.0 3.3 %copy-done = bf16[8,1024,400]{2,1,0:T(8,128)(2,1)} copy-done((bf16[8,1024,400]{2,1,0:T(8,128)(2,1)}, bf16[8,1024,400]{2,1,0:T(8,128)(2,1)S(1)}, u32[]{:S(2)}) %copy-start) | copy-done | bytes 6553624
  39.3 2.8 %copy-done.4 = bf16[1024,3200]{1,0:T(8,128)(2,1)} copy-done((bf16[1024,3200]{1,0:T(8,128)(2,1)}, bf16[1024,3200]{1,0:T(8,128)(2,1)S(1)}, u32[]{:S(2)}) %copy-start.4) | copy-done | bytes 6553624
  42.3 6.1 %all-gather.11.cloned.1.call-done = bf16[8,100,768]{2,1,0:T(8,128)(2,1)} async-done(((bf16[1,100,768]{2,1,0:T(8,128)(2,1)}), bf16[8,100,768]{2,1,0:T(8,128)(2,1)}) %all-gather.11.cloned.1.call-update) | async-done | bytes 1228816 | tf_op jit(solution)/shard_map/all_gather | solution.py:321
  48.3 1.4 fusion.1
  49.7 0.1 reshape.36.refs_1_
  49.8 0.1 reshape.37.refs_2_
  50.0 0.1 broadcast_in_dim.38.scale_ref
  50.1 1.3 collective-permute-start.4
  51.4 1.5 collective-permute-start.7
  52.9 2.7 %collective-permute-start.6 = (bf16[400,768]{1,0:T(8,128)(2,1)S(1)}, bf16[400,768]{1,0:T(8,128)(2,1)S(1)}, u32[]{:S(2)}, u32[]{:S(2)}) collective-permute-start(bf16[400,768]{1,0:T(8,128)(2,1)S(1)} %reshape.36.refs_1_), channel_id=1, source_target_pairs={{0,3},{1,0},{2,1},{3,2},{4,7},{5,4},{6,5},{7,6},{8,11},{9,8},{10,9... | collective-permute-start | bytes 1843208 | tf_op jit(solution)/shard_map/ppermute | solution.py:303
  55.5 6.7 %collective-permute-done.4.refs_3_ = bf16[400,768]{1,0:T(8,128)(2,1)S(1)} collective-permute-done((bf16[400,768]{1,0:T(8,128)(2,1)S(1)}, bf16[400,768]{1,0:T(8,128)(2,1)S(1)}, u32[]{:S(2)}, u32[]{:S(2)}) %collective-permute-start.4) | collective-permute-done | bytes 614432 | tf_op jit(solution)/shard_map/ppermute | solution.py:303
  62.3 2.7 %collective-permute-start.9 = (bf16[400,768]{1,0:T(8,128)(2,1)S(1)}, bf16[400,768]{1,0:T(8,128)(2,1)S(1)}, u32[]{:S(2)}, u32[]{:S(2)}) collective-permute-start(bf16[400,768]{1,0:T(8,128)(2,1)S(1)} %collective-permute-done.7.refs_6_), channel_id=1, source_target_pairs={{0,3},{1,0},{2,1},{3,2},{4,7},{5,4},{6,5},{7,6},{8,11},{9,8},{10,9... | collective-permute-start | bytes 1843208 | tf_op jit(solution)/shard_map/ppermute | solution.py:303
  64.9 3.4 %copy-done.1 = bf16[8,1024,400]{2,1,0:T(8,128)(2,1)S(1)} copy-done((bf16[8,1024,400]{2,1,0:T(8,128)(2,1)S(1)}, bf16[8,1024,400]{2,1,0:T(8,128)(2,1)}, u32[]{:S(2)}) %copy-start.1) | copy-done | bytes 6553624
  68.3 2.4 %shard_map.83.refs_0_ = f32[1024,768]{1,0:T(8,128)S(1)} custom-call(s32[1]{0:T(128)} %bitcast.12.at_ref, bf16[8,1024,400]{2,1,0:T(8,128)(2,1)S(1)} %copy-done.1, bf16[400,768]{1,0:T(8,128)(2,1)S(1)} %reshape.36.refs_1_, bf16[400,768]{1,0:T(8,128)(2,1)S(1)} %reshape.37.refs_2_), custom_call_target="tpu_custom_call" | custom-call | flops 1258291200 | bytes 10000000 | tf_op jit(solution)/shard_map/pallas_call | solution.py:72
  70.8 4.6 %collective-permute-done.5.refs_4_ = bf16[400,768]{1,0:T(8,128)(2,1)S(1)} collective-permute-done((bf16[400,768]{1,0:T(8,128)(2,1)S(1)}, bf16[400,768]{1,0:T(8,128)(2,1)S(1)}, u32[]{:S(2)}, u32[]{:S(2)}) %collective-permute-start.5) | collective-permute-done | bytes 614432 | tf_op jit(solution)/shard_map/ppermute | solution.py:303
  75.4 6.0 %shard_map.84.sums = f32[1024,768]{1,0:T(8,128)S(1)} custom-call(s32[2]{0:T(128)S(1)} %get-tuple-element.44.at_ref, f32[1024,768]{1,0:T(8,128)S(1)} %shard_map.83.refs_0_, bf16[8,1024,400]{2,1,0:T(8,128)(2,1)} %copy-done, bf16[8,1024,400]{2,1,0:T(8,128)(2,1)} %copy-done, bf16[400,768]{1,0:T(8,128)(2,1)S(1)} %collective-permute-done.4.refs_3_, ...), custom_call_target="tpu_custom_call" | custom-call | flops 2516582400 | bytes 10000000 | tf_op jit(solution)/shard_map/pallas_call | solution.py:72
  81.5 1.6 copy-done.2
  83.1 5.6 %collective-permute-done.8.top = bf16[400,768]{1,0:T(8,128)(2,1)S(1)} collective-permute-done((bf16[400,768]{1,0:T(8,128)(2,1)S(1)}, bf16[400,768]{1,0:T(8,128)(2,1)S(1)}, u32[]{:S(2)}, u32[]{:S(2)}) %collective-permute-start.8) | collective-permute-done | bytes 614432 | tf_op jit(solution)/shard_map/ppermute | solution.py:303
  88.7 2.5 %all-gather.7.cloned.1.call-done.w_ref = bf16[3200,384]{1,0:T(8,128)(2,1)} async-done(((bf16[400,384]{1,0:T(8,128)(2,1)}), bf16[3200,384]{1,0:T(8,128)(2,1)}) %all-gather.7.cloned.1.call-update) | async-done | bytes 2457616 | tf_op jit(solution)/shard_map/all_gather | solution.py:337
  91.2 14.4 %shard_map.85 = (bf16[1024,768]{1,0:T(8,128)(2,1)S(1)}, bf16[384,1024]{1,0:T(8,128)(2,1)S(1)}, bf16[384,512]{1,0:T(8,128)(2,1)S(1)}) custom-call(s32[9]{0:T(128)S(1)} %concatenate.31.at_ref, f32[1024,768]{1,0:T(8,128)} %copy-done.2, bf16[8,1024,400]{2,1,0:T(8,128)(2,1)} %copy-done, bf16[400,768]{1,0:T(8,128)(2,1)S(1)} %collective-permute-done.8.top, ...), custom_call_target="tpu_custom_call" | custom-call | flops 3951034368 | bytes 18000000 | tf_op jit(solution)/shard_map/pallas_call | solution.py:147
  105.7 1.3 collective-permute-start.10
  107.0 5.5 %collective-permute-start.12 = (bf16[384,512]{1,0:T(8,128)(2,1)S(1)}, bf16[384,512]{1,0:T(8,128)(2,1)S(1)}, u32[]{:S(2)}, u32[]{:S(2)}) collective-permute-start(bf16[384,512]{1,0:T(8,128)(2,1)S(1)} %get-tuple-element.52.refs_0_), channel_id=1, source_target_pairs={{0,24},{4,28},{8,0},{12,4},{16,8},{20,12},{24,16},{28,20},{1,25},{... | collective-permute-start | bytes 1179656 | tf_op jit(solution)/shard_map/ppermute | solution.py:303
  112.5 5.1 %shard_map.86.refs_0_ = bf16[384,512]{1,0:T(8,128)(2,1)S(1)} custom-call(s32[5]{0:T(128)S(1)} %pad_add_fusion.2.info_ref, bf16[1024,768]{1,0:T(8,128)(2,1)S(1)} %get-tuple-element.50.q0_ref.q1_ref.k_ref, bf16[1024,768]{1,0:T(8,128)(2,1)S(1)} %get-tuple-element.50.q0_ref.q1_ref.k_ref, bf16[1024,768]{1,0:T(8,128)(2,1)S(1)} %get-tuple-element.50.q0_ref.q1_ref.k_ref, ...), custom_call_target="tpu_custom_call" | custom-call | flops 805306368 | bytes 4000000 | tf_op jit(solution)/shard_map/pallas_call | solution.py:188
  117.6 1.5 collective-permute-done.10.refs_1_
  119.3 2.7 %collective-permute-start.13 = (bf16[576,512]{1,0:T(8,128)(2,1)S(1)}, bf16[576,512]{1,0:T(8,128)(2,1)S(1)}, u32[]{:S(2)}, u32[]{:S(2)}) collective-permute-start(bf16[576,512]{1,0:T(8,128)(2,1)S(1)} %get-tuple-element.73), channel_id=1, source_target_pairs={{0,24},{4,28},{8,0},{12,4},{16,8},{20,12},{24,16},{28,20},{1,25},{... | collective-permute-start | bytes 1769480 | tf_op jit(solution)/shard_map/ppermute | solution.py:303
  122.0 10.1 %collective-permute-done.11.refs_1_.refs_3_ = bf16[576,512]{1,0:T(8,128)(2,1)S(1)} collective-permute-done((bf16[576,512]{1,0:T(8,128)(2,1)S(1)}, bf16[576,512]{1,0:T(8,128)(2,1)S(1)}, u32[]{:S(2)}, u32[]{:S(2)}) %collective-permute-start.11) | collective-permute-done | bytes 589856 | tf_op jit(solution)/shard_map/ppermute | solution.py:303
  132.1 0.7 slice.68
  132.8 0.7 slice.69
  133.5 2.7 %collective-permute-start.15 = (bf16[192,512]{1,0:T(8,128)(2,1)}, bf16[192,512]{1,0:T(8,128)(2,1)S(1)}, u32[]{:S(2)}, u32[]{:S(2)}) collective-permute-start(bf16[192,512]{1,0:T(8,128)(2,1)} %slice.69), channel_id=1, source_target_pairs={{0,24},{4,28},{8,0},{12,4},{16,8},{20,12},{24,16},{28,20},{1,25},{... | collective-permute-start | bytes 589832 | tf_op jit(solution)/shard_map/ppermute | solution.py:303
  136.2 1.0 copy-done.6
  137.2 1.0 copy-done.8
  138.2 5.0 %shard_map.89 = (f32[400,512]{1,0:T(8,128)S(1)}, bf16[400,512]{1,0:T(8,128)(2,1)S(1)}) custom-call(s32[8]{0:T(128)S(1)} %stack.64.info_ref, bf16[384,512]{1,0:T(8,128)(2,1)S(1)} %copy-done.8, bf16[384,512]{1,0:T(8,128)(2,1)S(1)} %collective-permute-done.10.refs_1_, bf16[384,512]{1,0:T(8,128)(2,1)S(1)} %copy-done.6, ...), custom_call_target="tpu_custom_call" | custom-call | flops 1258291200 | bytes 6000000 | tf_op jit(solution)/shard_map/pallas_call | solution.py:238
  143.2 4.8 %collective-permute-start.20 = (bf16[400,512]{1,0:T(8,128)(2,1)S(1)}, bf16[400,512]{1,0:T(8,128)(2,1)S(1)}, u32[]{:S(2)}, u32[]{:S(2)}) collective-permute-start(bf16[400,512]{1,0:T(8,128)(2,1)S(1)} %get-tuple-element.64), channel_id=1, source_target_pairs={{0,4},{4,0},{8,12},{12,8},{16,20},{20,16},{24,28},{28,24},{1,5},{5... | collective-permute-start | bytes 1228808 | tf_op jit(solution)/shard_map/ppermute | solution.py:374
  148.0 5.0 %shard_map.87 = (f32[400,512]{1,0:T(8,128)S(1)}, bf16[400,512]{1,0:T(8,128)(2,1)S(1)}) custom-call(s32[8]{0:T(128)S(1)} %stack.64.info_ref, bf16[384,512]{1,0:T(8,128)(2,1)S(1)} %shard_map.86.refs_0_, bf16[576,512]{1,0:T(8,128)(2,1)S(1)} %collective-permute-done.11.refs_1_.refs_3_, bf16[576,512]{1,0:T(8,128)(2,1)S(1)} %collective-permute-done.13.refs_2_.refs_4_, ...), custom_call_target="tpu_custom_call" | custom-call | flops 1258291200 | bytes 6000000 | tf_op jit(solution)/shard_map/pallas_call | solution.py:238
  153.1 0.1 collective-permute-start.16
  153.2 0.8 shard_map.90
  154.0 1.1 collective-permute-start.21
  155.1 6.5 %collective-permute-start.22 = (bf16[400,128]{1,0:T(8,128)(2,1)S(1)}, bf16[400,128]{1,0:T(8,128)(2,1)S(1)}, u32[]{:S(2)}, u32[]{:S(2)}) collective-permute-start(bf16[400,128]{1,0:T(8,128)(2,1)S(1)} %get-tuple-element.66), channel_id=1, source_target_pairs={{0,128},{32,160},{64,192},{96,224},{128,0},{160,32},{192,64},{224,... | collective-permute-start | bytes 307208 | tf_op jit(solution)/shard_map/ppermute | solution.py:303
  161.6 2.5 %collective-permute-start.23 = (bf16[400,128]{1,0:T(8,128)(2,1)S(1)}, bf16[400,128]{1,0:T(8,128)(2,1)S(1)}, u32[]{:S(2)}, u32[]{:S(2)}) collective-permute-start(bf16[400,128]{1,0:T(8,128)(2,1)S(1)} %get-tuple-element.67), channel_id=1, source_target_pairs={{0,96},{32,128},{64,160},{96,192},{128,224},{160,0},{192,32},{224,... | collective-permute-start | bytes 307208 | tf_op jit(solution)/shard_map/ppermute | solution.py:303
  164.1 2.0 %collective-permute-start.24 = (bf16[400,128]{1,0:T(8,128)(2,1)S(1)}, bf16[400,128]{1,0:T(8,128)(2,1)S(1)}, u32[]{:S(2)}, u32[]{:S(2)}) collective-permute-start(bf16[400,128]{1,0:T(8,128)(2,1)S(1)} %get-tuple-element.68), channel_id=1, source_target_pairs={{0,160},{32,192},{64,224},{96,0},{128,32},{160,64},{192,96},{224,1... | collective-permute-start | bytes 307208 | tf_op jit(solution)/shard_map/ppermute | solution.py:303
  166.0 0.7 shard_map.88
  166.8 1.2 collective-permute-start.17
  167.9 1.6 collective-permute-start.18
  169.5 7.5 %collective-permute-start.19 = (bf16[400,128]{1,0:T(8,128)(2,1)S(1)}, bf16[400,128]{1,0:T(8,128)(2,1)S(1)}, u32[]{:S(2)}, u32[]{:S(2)}) collective-permute-start(bf16[400,128]{1,0:T(8,128)(2,1)S(1)} %get-tuple-element.61), channel_id=1, source_target_pairs={{0,192},{32,224},{64,0},{96,32},{128,64},{160,96},{192,128},{224,1... | collective-permute-start | bytes 307208 | tf_op jit(solution)/shard_map/ppermute | solution.py:303
  177.1 0.4 collective-permute-done.17.refs_1_
  177.5 0.3 collective-permute-done.18.refs_2_
  177.8 4.8 %collective-permute-done.19.refs_3_ = bf16[400,128]{1,0:T(8,128)(2,1)S(1)} collective-permute-done((bf16[400,128]{1,0:T(8,128)(2,1)S(1)}, bf16[400,128]{1,0:T(8,128)(2,1)S(1)}, u32[]{:S(2)}, u32[]{:S(2)}) %collective-permute-start.19) | collective-permute-done | bytes 102432 | tf_op jit(solution)/shard_map/ppermute | solution.py:303
  182.6 1.6 shard_map.91
  (62 shorter events, 1.0 us)
Async XLA Ops:
  6.5 41.8 %all-gather.11.cloned.1.call-start = ((), (), s32[]{:S(2)}) async-start(), calls=%async_computation.2 | async-start | bytes 1437696 | tf_op jit(solution)/shard_map/all_gather | solution.py:321
  8.2 83.0 %all-gather.7.cloned.1.call-start = ((), (), s32[]{:S(2)}) async-start(), calls=%async_computation | async-start | bytes 2764800 | tf_op jit(solution)/shard_map/all_gather | solution.py:337
  8.3 1.5 collective-permute-start
  9.8 6.1 %collective-permute-start.1 = (bf16[100,768]{1,0:T(8,128)(2,1)S(1)}, bf16[100,768]{1,0:T(8,128)(2,1)S(1)}, u32[]{:S(2)}, u32[]{:S(2)}) collective-permute-start(bf16[100,768]{1,0:T(8,128)(2,1)S(1)} %pad_maximum_fusion.2), channel_id=1, source_target_pairs={{0,1},{1,2},{2,3},{3,0},{4,5},{5,6},{6,7},{7,4},{8,9},{9,10},{10,1... | collective-permute-start | bytes 460808 | tf_op jit(solution)/shard_map/ppermute | solution.py:303
  12.0 4.1 %collective-permute-start.2 = (bf16[100,768]{1,0:T(8,128)(2,1)S(1)}, bf16[100,768]{1,0:T(8,128)(2,1)S(1)}, u32[]{:S(2)}, u32[]{:S(2)}) collective-permute-start(bf16[100,768]{1,0:T(8,128)(2,1)S(1)} %pad_maximum_fusion.2), channel_id=1, source_target_pairs={{0,3},{1,0},{2,1},{3,2},{4,7},{5,4},{6,5},{7,6},{8,11},{9,8},{10,9... | collective-permute-start | bytes 460808 | tf_op jit(solution)/shard_map/ppermute | solution.py:303
  13.4 7.2 %collective-permute-start.3 = (bf16[100,768]{1,0:T(8,128)(2,1)S(1)}, bf16[100,768]{1,0:T(8,128)(2,1)S(1)}, u32[]{:S(2)}, u32[]{:S(2)}) collective-permute-start(bf16[100,768]{1,0:T(8,128)(2,1)S(1)} %pad_maximum_fusion.2), channel_id=1, source_target_pairs={{0,2},{1,3},{2,0},{3,1},{4,6},{5,7},{6,4},{7,5},{8,10},{9,11},{10,... | collective-permute-start | bytes 460808 | tf_op jit(solution)/shard_map/ppermute | solution.py:303
  21.6 3.3 %copy-start.10 = (f32[3200]{0:T(1024)S(1)}, f32[3200]{0:T(1024)}, u32[]{:S(2)}) copy-start(f32[3200]{0:T(1024)} %param.10) | copy-start | bytes 38404
  21.6 3.3 %copy-start.12 = (s32[8]{0:T(128)S(1)}, s32[8]{0:T(128)}, u32[]{:S(2)}) copy-start(s32[8]{0:T(128)} %constant.105.clone) | copy-start | bytes 100
  21.7 114.5 %all-gather.9.cloned.1.call-start = ((), (), s32[]{:S(2)}) async-start(), calls=%async_computation.1 | async-start | bytes 2764800 | tf_op jit(solution)/shard_map/all_gather | solution.py:355
  25.9 2.9 %copy-start.3 = (bf16[1,1024,3200]{2,1,0:T(8,128)(2,1)S(1)}, bf16[1,1024,3200]{2,1,0:T(8,128)(2,1)}, u32[]{:S(2)}) copy-start(bf16[1,1024,3200]{2,1,0:T(8,128)(2,1)} %param.8) | copy-start | bytes 19660804
  36.0 3.3 %copy-start = (bf16[8,1024,400]{2,1,0:T(8,128)(2,1)}, bf16[8,1024,400]{2,1,0:T(8,128)(2,1)S(1)}, u32[]{:S(2)}) copy-start(bf16[8,1024,400]{2,1,0:T(8,128)(2,1)S(1)} %get-tuple-element.46.refs_0_.refs_1_.refs_2_.x_ref) | copy-start | bytes 19660804
  39.3 2.8 %copy-start.4 = (bf16[1024,3200]{1,0:T(8,128)(2,1)}, bf16[1024,3200]{1,0:T(8,128)(2,1)S(1)}, u32[]{:S(2)}) copy-start(bf16[1024,3200]{1,0:T(8,128)(2,1)S(1)} %get-tuple-element.49.normed) | copy-start | bytes 19660804
  42.3 7.7 %copy-start.11 = (f32[400]{0:T(512)S(1)}, f32[400]{0:T(512)}, u32[]{:S(2)}) copy-start(f32[400]{0:T(512)} %param.13) | copy-start | bytes 4804
  50.1 12.2 %collective-permute-start.4 = (bf16[400,768]{1,0:T(8,128)(2,1)S(1)}, bf16[400,768]{1,0:T(8,128)(2,1)S(1)}, u32[]{:S(2)}, u32[]{:S(2)}) collective-permute-start(bf16[400,768]{1,0:T(8,128)(2,1)S(1)} %reshape.36.refs_1_), channel_id=1, source_target_pairs={{0,1},{1,2},{2,3},{3,0},{4,5},{5,6},{6,7},{7,4},{8,9},{9,10},{10,1... | collective-permute-start | bytes 1843208 | tf_op jit(solution)/shard_map/ppermute | solution.py:303
  51.4 10.9 %collective-permute-start.7 = (bf16[400,768]{1,0:T(8,128)(2,1)S(1)}, bf16[400,768]{1,0:T(8,128)(2,1)S(1)}, u32[]{:S(2)}, u32[]{:S(2)}) collective-permute-start(bf16[400,768]{1,0:T(8,128)(2,1)S(1)} %reshape.37.refs_2_), channel_id=1, source_target_pairs={{0,3},{1,0},{2,1},{3,2},{4,7},{5,4},{6,5},{7,6},{8,11},{9,8},{10,9... | collective-permute-start | bytes 1843208 | tf_op jit(solution)/shard_map/ppermute | solution.py:303
  52.9 22.6 %collective-permute-start.5 = (bf16[400,768]{1,0:T(8,128)(2,1)S(1)}, bf16[400,768]{1,0:T(8,128)(2,1)S(1)}, u32[]{:S(2)}, u32[]{:S(2)}) collective-permute-start(bf16[400,768]{1,0:T(8,128)(2,1)S(1)} %reshape.37.refs_2_), channel_id=1, source_target_pairs={{0,1},{1,2},{2,3},{3,0},{4,5},{5,6},{6,7},{7,4},{8,9},{9,10},{10,1... | collective-permute-start | bytes 1843208 | tf_op jit(solution)/shard_map/ppermute | solution.py:303
  52.9 22.6 %collective-permute-start.6 = (bf16[400,768]{1,0:T(8,128)(2,1)S(1)}, bf16[400,768]{1,0:T(8,128)(2,1)S(1)}, u32[]{:S(2)}, u32[]{:S(2)}) collective-permute-start(bf16[400,768]{1,0:T(8,128)(2,1)S(1)} %reshape.36.refs_1_), channel_id=1, source_target_pairs={{0,3},{1,0},{2,1},{3,2},{4,7},{5,4},{6,5},{7,6},{8,11},{9,8},{10,9... | collective-permute-start | bytes 1843208 | tf_op jit(solution)/shard_map/ppermute | solution.py:303
  62.3 26.4 %collective-permute-start.8 = (bf16[400,768]{1,0:T(8,128)(2,1)S(1)}, bf16[400,768]{1,0:T(8,128)(2,1)S(1)}, u32[]{:S(2)}, u32[]{:S(2)}) collective-permute-start(bf16[400,768]{1,0:T(8,128)(2,1)S(1)} %collective-permute-done.4.refs_3_), channel_id=1, source_target_pairs={{0,1},{1,2},{2,3},{3,0},{4,5},{5,6},{6,7},{7,4},{8,9},{9,10},{10,1... | collective-permute-start | bytes 1843208 | tf_op jit(solution)/shard_map/ppermute | solution.py:303
  62.3 26.4 %collective-permute-start.9 = (bf16[400,768]{1,0:T(8,128)(2,1)S(1)}, bf16[400,768]{1,0:T(8,128)(2,1)S(1)}, u32[]{:S(2)}, u32[]{:S(2)}) collective-permute-start(bf16[400,768]{1,0:T(8,128)(2,1)S(1)} %collective-permute-done.7.refs_6_), channel_id=1, source_target_pairs={{0,3},{1,0},{2,1},{3,2},{4,7},{5,4},{6,5},{7,6},{8,11},{9,8},{10,9... | collective-permute-start | bytes 1843208 | tf_op jit(solution)/shard_map/ppermute | solution.py:303
  64.9 3.4 %copy-start.1 = (bf16[8,1024,400]{2,1,0:T(8,128)(2,1)S(1)}, bf16[8,1024,400]{2,1,0:T(8,128)(2,1)}, u32[]{:S(2)}) copy-start(bf16[8,1024,400]{2,1,0:T(8,128)(2,1)} %copy-done) | copy-start | bytes 19660804
  81.5 1.7 copy-start.2
  105.7 11.9 %copy-start.7 = (bf16[384,512]{1,0:T(8,128)(2,1)}, bf16[384,512]{1,0:T(8,128)(2,1)S(1)}, u32[]{:S(2)}) copy-start(bf16[384,512]{1,0:T(8,128)(2,1)S(1)} %get-tuple-element.52.refs_0_) | copy-start | bytes 1179652
  105.7 13.4 %collective-permute-start.10 = (bf16[384,512]{1,0:T(8,128)(2,1)S(1)}, bf16[384,512]{1,0:T(8,128)(2,1)S(1)}, u32[]{:S(2)}, u32[]{:S(2)}) collective-permute-start(bf16[384,512]{1,0:T(8,128)(2,1)S(1)} %get-tuple-element.52.refs_0_), channel_id=1, source_target_pairs={{0,8},{4,12},{8,16},{12,20},{16,24},{20,28},{24,0},{28,4},{1,9},{5... | collective-permute-start | bytes 1179656 | tf_op jit(solution)/shard_map/ppermute | solution.py:303
  107.0 12.1 %collective-permute-start.12 = (bf16[384,512]{1,0:T(8,128)(2,1)S(1)}, bf16[384,512]{1,0:T(8,128)(2,1)S(1)}, u32[]{:S(2)}, u32[]{:S(2)}) collective-permute-start(bf16[384,512]{1,0:T(8,128)(2,1)S(1)} %get-tuple-element.52.refs_0_), channel_id=1, source_target_pairs={{0,24},{4,28},{8,0},{12,4},{16,8},{20,12},{24,16},{28,20},{1,25},{... | collective-permute-start | bytes 1179656 | tf_op jit(solution)/shard_map/ppermute | solution.py:303
  119.1 13.7 %copy-start.5 = (bf16[384,512]{1,0:T(8,128)(2,1)}, bf16[384,512]{1,0:T(8,128)(2,1)S(1)}, u32[]{:S(2)}) copy-start(bf16[384,512]{1,0:T(8,128)(2,1)S(1)} %collective-permute-done.12.refs_2_) | copy-start | bytes 1179652
  119.2 12.9 %collective-permute-start.11 = (bf16[576,512]{1,0:T(8,128)(2,1)S(1)}, bf16[576,512]{1,0:T(8,128)(2,1)S(1)}, u32[]{:S(2)}, u32[]{:S(2)}) collective-permute-start(bf16[576,512]{1,0:T(8,128)(2,1)S(1)} %get-tuple-element.74), channel_id=1, source_target_pairs={{0,8},{4,12},{8,16},{12,20},{16,24},{20,28},{24,0},{28,4},{1,9},{5... | collective-permute-start | bytes 1769480 | tf_op jit(solution)/shard_map/ppermute | solution.py:303
  119.3 13.5 %collective-permute-start.13 = (bf16[576,512]{1,0:T(8,128)(2,1)S(1)}, bf16[576,512]{1,0:T(8,128)(2,1)S(1)}, u32[]{:S(2)}, u32[]{:S(2)}) collective-permute-start(bf16[576,512]{1,0:T(8,128)(2,1)S(1)} %get-tuple-element.73), channel_id=1, source_target_pairs={{0,24},{4,28},{8,0},{12,4},{16,8},{20,12},{24,16},{28,20},{1,25},{... | collective-permute-start | bytes 1769480 | tf_op jit(solution)/shard_map/ppermute | solution.py:303
  132.8 15.2 %collective-permute-start.14 = (bf16[192,512]{1,0:T(8,128)(2,1)}, bf16[192,512]{1,0:T(8,128)(2,1)S(1)}, u32[]{:S(2)}, u32[]{:S(2)}) collective-permute-start(bf16[192,512]{1,0:T(8,128)(2,1)} %slice.68), channel_id=1, source_target_pairs={{0,8},{4,12},{8,16},{12,20},{16,24},{20,28},{24,0},{28,4},{1,9},{5... | collective-permute-start | bytes 589832 | tf_op jit(solution)/shard_map/ppermute | solution.py:303
  133.5 14.5 %collective-permute-start.15 = (bf16[192,512]{1,0:T(8,128)(2,1)}, bf16[192,512]{1,0:T(8,128)(2,1)S(1)}, u32[]{:S(2)}, u32[]{:S(2)}) collective-permute-start(bf16[192,512]{1,0:T(8,128)(2,1)} %slice.69), channel_id=1, source_target_pairs={{0,24},{4,28},{8,0},{12,4},{16,8},{20,12},{24,16},{28,20},{1,25},{... | collective-permute-start | bytes 589832 | tf_op jit(solution)/shard_map/ppermute | solution.py:303
  136.2 1.0 copy-start.6
  137.2 1.0 copy-start.8
  143.2 10.0 %collective-permute-start.20 = (bf16[400,512]{1,0:T(8,128)(2,1)S(1)}, bf16[400,512]{1,0:T(8,128)(2,1)S(1)}, u32[]{:S(2)}, u32[]{:S(2)}) collective-permute-start(bf16[400,512]{1,0:T(8,128)(2,1)S(1)} %get-tuple-element.64), channel_id=1, source_target_pairs={{0,4},{4,0},{8,12},{12,8},{16,20},{20,16},{24,28},{28,24},{1,5},{5... | collective-permute-start | bytes 1228808 | tf_op jit(solution)/shard_map/ppermute | solution.py:374
  153.1 29.5 %copy-start.9 = (s32[4,8]{1,0:T(4,128)S(1)}, s32[4,8]{1,0:T(4,128)}, u32[]{:S(2)}) copy-start(s32[4,8]{1,0:T(4,128)} %order_ref.1) | copy-start | bytes 388
  153.1 12.9 %collective-permute-start.16 = (bf16[400,512]{1,0:T(8,128)(2,1)S(1)}, bf16[400,512]{1,0:T(8,128)(2,1)S(1)}, u32[]{:S(2)}, u32[]{:S(2)}) collective-permute-start(bf16[400,512]{1,0:T(8,128)(2,1)S(1)} %get-tuple-element.55), channel_id=1, source_target_pairs={{0,4},{4,0},{8,12},{12,8},{16,20},{20,16},{24,28},{28,24},{1,5},{5... | collective-permute-start | bytes 1228808 | tf_op jit(solution)/shard_map/ppermute | solution.py:374
  154.0 13.9 %collective-permute-start.21 = (bf16[400,128]{1,0:T(8,128)(2,1)S(1)}, bf16[400,128]{1,0:T(8,128)(2,1)S(1)}, u32[]{:S(2)}, u32[]{:S(2)}) collective-permute-start(bf16[400,128]{1,0:T(8,128)(2,1)S(1)} %get-tuple-element.65), channel_id=1, source_target_pairs={{0,64},{32,96},{64,128},{96,160},{128,192},{160,224},{192,0},{224,... | collective-permute-start | bytes 307208 | tf_op jit(solution)/shard_map/ppermute | solution.py:303
  155.1 14.5 %collective-permute-start.22 = (bf16[400,128]{1,0:T(8,128)(2,1)S(1)}, bf16[400,128]{1,0:T(8,128)(2,1)S(1)}, u32[]{:S(2)}, u32[]{:S(2)}) collective-permute-start(bf16[400,128]{1,0:T(8,128)(2,1)S(1)} %get-tuple-element.66), channel_id=1, source_target_pairs={{0,128},{32,160},{64,192},{96,224},{128,0},{160,32},{192,64},{224,... | collective-permute-start | bytes 307208 | tf_op jit(solution)/shard_map/ppermute | solution.py:303
  161.6 15.5 %collective-permute-start.23 = (bf16[400,128]{1,0:T(8,128)(2,1)S(1)}, bf16[400,128]{1,0:T(8,128)(2,1)S(1)}, u32[]{:S(2)}, u32[]{:S(2)}) collective-permute-start(bf16[400,128]{1,0:T(8,128)(2,1)S(1)} %get-tuple-element.67), channel_id=1, source_target_pairs={{0,96},{32,128},{64,160},{96,192},{128,224},{160,0},{192,32},{224,... | collective-permute-start | bytes 307208 | tf_op jit(solution)/shard_map/ppermute | solution.py:303
  164.1 13.0 %collective-permute-start.24 = (bf16[400,128]{1,0:T(8,128)(2,1)S(1)}, bf16[400,128]{1,0:T(8,128)(2,1)S(1)}, u32[]{:S(2)}, u32[]{:S(2)}) collective-permute-start(bf16[400,128]{1,0:T(8,128)(2,1)S(1)} %get-tuple-element.68), channel_id=1, source_target_pairs={{0,160},{32,192},{64,224},{96,0},{128,32},{160,64},{192,96},{224,1... | collective-permute-start | bytes 307208 | tf_op jit(solution)/shard_map/ppermute | solution.py:303
  166.8 10.7 %collective-permute-start.17 = (bf16[400,128]{1,0:T(8,128)(2,1)S(1)}, bf16[400,128]{1,0:T(8,128)(2,1)S(1)}, u32[]{:S(2)}, u32[]{:S(2)}) collective-permute-start(bf16[400,128]{1,0:T(8,128)(2,1)S(1)} %get-tuple-element.59), channel_id=1, source_target_pairs={{0,32},{32,64},{64,96},{96,128},{128,160},{160,192},{192,224},{224... | collective-permute-start | bytes 307208 | tf_op jit(solution)/shard_map/ppermute | solution.py:303
  167.9 9.9 %collective-permute-start.18 = (bf16[400,128]{1,0:T(8,128)(2,1)S(1)}, bf16[400,128]{1,0:T(8,128)(2,1)S(1)}, u32[]{:S(2)}, u32[]{:S(2)}) collective-permute-start(bf16[400,128]{1,0:T(8,128)(2,1)S(1)} %get-tuple-element.60), channel_id=1, source_target_pairs={{0,224},{32,0},{64,32},{96,64},{128,96},{160,128},{192,160},{224,1... | collective-permute-start | bytes 307208 | tf_op jit(solution)/shard_map/ppermute | solution.py:303
  169.5 13.0 %collective-permute-start.19 = (bf16[400,128]{1,0:T(8,128)(2,1)S(1)}, bf16[400,128]{1,0:T(8,128)(2,1)S(1)}, u32[]{:S(2)}, u32[]{:S(2)}) collective-permute-start(bf16[400,128]{1,0:T(8,128)(2,1)S(1)} %get-tuple-element.61), channel_id=1, source_target_pairs={{0,192},{32,224},{64,0},{96,32},{128,64},{160,96},{192,128},{224,1... | collective-permute-start | bytes 307208 | tf_op jit(solution)/shard_map/ppermute | solution.py:303
Sparse Core Ops, SparseCore 0:
  9.1 39.1 all-gather.10
  50.1 41.0 all-gather.6
  93.0 40.5 all-gather.8
